TPU v7x, 128 devices: a whole 4x4x4 slice. The times are simulated.
128 devices in a mesh: space: 64 (over x, y_lo, z, core), head: 2 (over y_hi).
Axes of the slice: x: 4, y: 4 (y_hi: 2, y_lo: 2; y = y_hi * 2 + y_lo), z: 4, core: 2. Of those that a mesh axis runs over, the one named last changes fastest.
Arguments:
- grid_feat: bfloat16 [131072, 1024], P('space', 'head'), may hold values from -6 to 6
- mesh_feat: bfloat16 [8192, 1024], P('space', 'head'), may hold values from -6 to 6
- edge_src: int32 [8192, 16], P('space'), may hold values from 0 to 131071, as said below
- degree: int32 [8192], P('space'), may hold values from 8 to 16
- offsets: int32 [16], replicated, may hold values from -32 to 32, as said below
- w_kv: bfloat16 [2, 1024, 1024], P(None, None, 'head'), may hold values from -0.1875 to 0.1875
- w_query: bfloat16 [1024, 1024], P(None, 'head'), may hold values from -0.1875 to 0.1875
- w_out: bfloat16 [1024, 1024], P('head'), may hold values from -0.1875 to 0.1875
- w_mesh: bfloat16 [3, 1024, 1024], P(None, None, 'head'), may hold values from -0.1875 to 0.1875
- w_mesh_out: bfloat16 [1024, 1024], P('head'), may hold values from -0.1875 to 0.1875
- cotangent: bfloat16 [8192, 1024], P('space', 'head'), may hold values from -6 to 6
Outputs:
- encoded: bfloat16 [8192, 1024], P('space', 'head')
- mesh_out: bfloat16 [8192, 1024], P('space', 'head')
- grad_grid: bfloat16 [131072, 1024], P('space', 'head')
- grad_kv: float32 [2, 1024, 1024], P(None, None, 'head')
Inputs may be any that keep to these rules, and one draw needn't show every extreme that they name: `edge_src`: an edge of a mesh node of shard s (nodes s*128 to (s+1)*128 - 1) comes from grid rows s*2048 - 128 to (s+1)*2048 + 127 inside the grid; the first node of every shard but the first reaches the lowest of these rows and the last node of every shard but the last the highest. Slots at and after degree are padding. 16 distinct offsets that include -32 and 32.
All inputs are finite; a program needn't handle non-finite values.
Results may differ from a plain program's by a relative error of at most 0.02.
Values may be sent and summed in bfloat16 or wider, within the bound.
A program may use at most 128 MiB of HBM per device.

v0:
```python
import math

import jax
import jax.numpy as jnp
from jax import lax
from jax.sharding import PartitionSpec as P

HEAD_SIZE = 64
RIM = 128
R = 32


score_cap = 3.0


def with_halo(block, sides, width):
    for axis, dim in sides:
        count = lax.axis_size(axis)
        forward = [(i, i + 1) for i in range(count - 1)]
        backward = [(target, source) for source, target in forward]
        low = lax.ppermute(
            lax.slice_in_dim(block, block.shape[dim] - width, None, axis=dim), axis, forward
        )
        high = lax.ppermute(lax.slice_in_dim(block, 0, width, axis=dim), axis, backward)
        block = jnp.concatenate([low, block, high], axis=dim)
    return block


def shifted(block, axis, distance):
    devices = range(lax.axis_size(axis))
    route = [(i - distance, i) for i in devices if i - distance in devices]
    return lax.ppermute(block, axis, route)


def local_attention(query, kv_rows, live):
    rows, slots, doubled = kv_rows.shape
    width = doubled // 2
    local_heads = width // HEAD_SIZE
    key_rows = kv_rows[:, :, :width].reshape(rows, slots, local_heads, HEAD_SIZE)
    value_rows = kv_rows[:, :, width:].reshape(rows, slots, local_heads, HEAD_SIZE)
    query_heads = query.reshape(rows, local_heads, HEAD_SIZE)
    raw_scores = jnp.einsum(
        "nzi,ngzi->ngz", query_heads, key_rows, preferred_element_type=jnp.float32
    ) / math.sqrt(HEAD_SIZE)
    capped = score_cap * jnp.tanh(raw_scores / score_cap)
    weights = jnp.where(live[:, :, None], jnp.exp(capped), 0.0)
    prob = weights / jnp.sum(weights, axis=1, keepdims=True)
    prob_matrix = prob.astype(jnp.bfloat16)
    attention_weights = jnp.einsum(
        "ztg,ztgw->zgw", prob_matrix, value_rows, preferred_element_type=jnp.float32
    )
    return (
        attention_weights.reshape(rows, width).astype(jnp.bfloat16),
        prob,
        prob_matrix,
        capped,
        value_rows,
    )


def shards(
    grid_feat,
    mesh_feat,
    edge_src,
    degree,
    offsets,
    w_kv,
    w_query,
    w_out,
    w_mesh,
    w_mesh_out,
    cotangent,
):
    space_index = lax.axis_index("space")
    g_dev = grid_feat.shape[0]
    m_dev = mesh_feat.shape[0]
    slots = edge_src.shape[1]
    width = w_query.shape[1]
    local_heads = width // HEAD_SIZE
    w_both = jnp.concatenate((w_kv[0], w_kv[1]), axis=1)
    grid_full, mesh_full = (
        lax.all_gather(grid_feat, "head", axis=1, tiled=True),
        lax.all_gather(mesh_feat, "head", axis=1, tiled=True),
    )
    kv_local = jnp.dot(grid_full, w_both, preferred_element_type=jnp.float32).astype(jnp.bfloat16)
    kv_wide = with_halo(kv_local, (("space", 0),), RIM)
    query = jnp.dot(mesh_full, w_query, preferred_element_type=jnp.float32).astype(jnp.bfloat16)
    wide_index = edge_src - (space_index * g_dev - RIM)
    live = jnp.arange(slots, dtype=jnp.int32)[None, :] < degree[:, None]
    attention_weights, prob, prob_matrix, capped, value_rows = local_attention(
        query, kv_wide[wide_index], live
    )
    partial_value = jnp.dot(attention_weights, w_out, preferred_element_type=jnp.float32)
    share = lax.psum_scatter(partial_value, "head", scatter_dimension=1, tiled=True)
    encoded = (mesh_feat.astype(jnp.float32) + share).astype(jnp.bfloat16)
    enc_full = lax.all_gather(encoded, "head", axis=1, tiled=True)
    mesh_q = jnp.dot(enc_full, w_mesh[0], preferred_element_type=jnp.float32).astype(jnp.bfloat16)
    mesh_kv = jnp.dot(
        enc_full,
        jnp.concatenate((w_mesh[1], w_mesh[2]), axis=1),
        preferred_element_type=jnp.float32,
    ).astype(jnp.bfloat16)
    mesh_wide = with_halo(mesh_kv, (("space", 0),), R)
    local_pos = jnp.arange(m_dev, dtype=jnp.int32)[:, None] + offsets[None, :]
    global_pos = space_index * m_dev + local_pos
    valid = (global_pos >= 0) & (global_pos < m_dev * lax.axis_size("space"))
    matt, unused_prob, unused_pb, unused_capped, unused_values = local_attention(
        mesh_q, mesh_wide[local_pos + R], valid
    )
    mesh_share = lax.psum_scatter(
        jnp.dot(matt, w_mesh_out, preferred_element_type=jnp.float32).astype(jnp.bfloat16),
        "head",
        scatter_dimension=1,
        tiled=True,
    ).astype(jnp.float32)
    mesh_out = (encoded.astype(jnp.float32) + mesh_share).astype(jnp.bfloat16)
    cot_full = lax.all_gather(cotangent, "head", axis=1, tiled=True)
    d_att = lax.dot_general(
        cot_full, w_out, (((1,), (1,)), ((), ())), preferred_element_type=jnp.float32
    ).astype(jnp.bfloat16)
    head_width = d_att.reshape(m_dev, local_heads, HEAD_SIZE)
    prob_gradient = jnp.einsum(
        "nzi,ngzi->ngz", head_width, value_rows, preferred_element_type=jnp.float32
    )
    ds = prob * (prob_gradient - jnp.sum(prob * prob_gradient, axis=1, keepdims=True))
    dr = ds * (1.0 - (capped / score_cap) ** 2) / math.sqrt(HEAD_SIZE)
    query_heads = query.reshape(m_dev, local_heads, HEAD_SIZE).astype(jnp.float32)
    dk_edges = (dr[:, :, :, None] * query_heads[:, None, :, :]).reshape(m_dev * slots, width)
    dv_edges = (
        prob_matrix.astype(jnp.float32)[:, :, :, None]
        * head_width.astype(jnp.float32)[:, None, :, :]
    ).reshape(m_dev * slots, width)
    edge_grads = jnp.concatenate((dk_edges, dv_edges), axis=1)
    wide_grads = jax.ops.segment_sum(
        edge_grads, wide_index.reshape(m_dev * slots), num_segments=g_dev + 2 * RIM
    )
    from_below = shifted(wide_grads[g_dev + RIM :].astype(jnp.bfloat16), "space", 1).astype(
        jnp.float32
    )
    from_above = shifted(wide_grads[:RIM].astype(jnp.bfloat16), "space", -1).astype(jnp.float32)
    owned = wide_grads[RIM : RIM + g_dev]
    owned = owned.at[:RIM].add(from_below).at[g_dev - RIM :].add(from_above)
    grads_low = owned.astype(jnp.bfloat16)
    weight_terms = lax.dot_general(
        grid_full, grads_low, (((0,), (0,)), ((), ())), preferred_element_type=jnp.float32
    )
    stacked = jnp.stack((weight_terms[:, :width], weight_terms[:, width:]))
    grad_kv = lax.psum(stacked, "space")
    grid_terms = lax.dot_general(
        grads_low, w_both, (((1,), (1,)), ((), ())), preferred_element_type=jnp.float32
    )
    grid_share = lax.psum_scatter(
        grid_terms.astype(jnp.bfloat16), "head", scatter_dimension=1, tiled=True
    )
    return (encoded, mesh_out, grid_share, grad_kv)


def solution(mesh):
    in_specs = (
        P("space", "head"),
        P("space", "head"),
        P("space", None),
        P("space"),
        P(),
        P(None, None, "head"),
        P(None, "head"),
        P("head", None),
        P(None, None, "head"),
        P("head", None),
        P("space", "head"),
    )
    out_specs = (P("space", "head"), P("space", "head"), P("space", "head"), P(None, None, "head"))
    return jax.shard_map(shards, mesh=mesh, in_specs=in_specs, out_specs=out_specs, check_vma=False)
```

profile of v0, /device:TPU:1, one launch (start us, length us, event | category | flops | bytes accessed | tf_op | source)
XLA Modules:
  0.0 942.9 jit_solution(10982052718660518236)
XLA Ops:
  9.6 7.7 all_gather.15
  17.9 6.0 all_gather.13
  29.2 44.6 %all-gather.2.cloned.1.call-done = bf16[2048,1024]{1,0:T(8,128)(2,1)} async-done(((bf16[2048,512]{1,0:T(8,128)(2,1)}), bf16[2048,1024]{1,0:T(8,128)(2,1)}) %all-gather.2.cloned.1.call-update) | async-done | bytes 4194320 | tf_op jit(solution)/shard_map/all_gather | solution.py:82
  73.7 7.1 convert_bitcast_fusion
  99.3 6.7 copy.21
  106.0 13.9 %gather_fusion = bf16[2048,1024]{1,0:T(8,128)(2,1)} fusion(bf16[2304,1024]{1,0:T(8,128)(2,1)} %copy.21, s32[2048]{0:T(1024)S(1)} %broadcast_clamp_fusion.1), kind=kCustom, calls=%fused_computation | custom fusion | bytes 8396800 | tf_op jit(solution)/shard_map/gather | solution.py:91
  119.9 4.7 fusion.55
  144.6 6.2 broadcast_multiply_fusion
  150.8 7.5 mul.71
  161.3 4.5 broadcast_multiply_fusion.1
  165.9 7.5 mul.67
  173.4 22.8 %scatter_custom_fusion = f32[2304,1024]{1,0:T(8,128)} fusion(s32[2048]{0:T(1024)S(1)} %reshape.210, f32[2048,512]{1,0:T(8,128)} %mul.71, f32[]{:T(128)} %constant.102, f32[2048,512]{1,0:T(8,128)} %mul.67, f32[]{:T(128)} %constant.89.clone.1), kind=kCustom, calls=%fused_computation.6 | custom fusion | flops 4194304 | bytes 17825800 | tf_op jit(solution)/shard_map/scatter-add | solution.py:134
  208.7 8.3 slice.127
  221.1 11.2 %convolution_bitcast_fusion = f32[1024,1024]{0,1:T(8,128)} fusion(bf16[2048,1024]{1,0:T(8,128)(2,1)} %all-gather.2.cloned.1.call-done, f32[2048,1024]{1,0:T(8,128)} %fusion.31), kind=kOutput, calls=%fused_computation.22 | convolution fusion | flops 4297064448 | bytes 16777216 | tf_op jit(solution)/shard_map/dot_general | solution.py:144
  232.3 7.9 reduce-scatter.4.cloned.1.call-done
  241.2 6.5 all_gather.14
  249.9 4.6 collective-permute-start.2
  260.1 9.9 %gather_fusion.1 = bf16[2048,1024]{1,0:T(8,128)(2,1)} fusion(bf16[192,1024]{1,0:T(8,128)(2,1)S(1)} %pad_maximum_fusion.5, s32[2048]{0:T(1024)S(1)} %broadcast_clamp_fusion), kind=kCustom, calls=%fused_computation.1 | custom fusion | bytes 8396800 | tf_op jit(solution)/shard_map/gather | solution.py:108
  270.0 4.7 fusion.54
  279.4 11.8 %fusion.22 = f32[128,8,16]{1,2,0:T(8,128)S(1)} fusion(f32[128,8,16]{1,2,0:T(8,128)S(1)} %copy.54, pred[128,16]{1,0:T(8,128)(4,1)S(1)} %copy-done.15), kind=kOutput, calls=%fused_computation.40 | output fusion | flops 99343 | bytes 133120 | tf_op jit(solution)/shard_map/div | solution.py:47
  303.1 9.6 %convolution_convert_fusion = bf16[2048,1024]{1,0:T(8,128)(2,1)} fusion(f32[2048,1024]{1,0:T(8,128)} %fusion.31, bf16[1024,512]{1,0:T(8,128)(2,1)S(1)} %copy-done.11, bf16[1024,512]{1,0:T(8,128)(2,1)S(1)} %copy-done.10), kind=kOutput, calls=%fused_computation.21 | convolution fusion | flops 4303355904 | bytes 14680064 | tf_op jit(solution)/shard_map/dot_general | solution.py:149
  315.6 558.9 %all-reduce.2.cloned.1.call-done = f32[2,1024,512]{1,2,0:T(8,128)} async-done(((f32[2,1024,512]{1,2,0:T(8,128)}), f32[2,1024,512]{1,2,0:T(8,128)}) %all-reduce.2.cloned.1.call-update) | async-done | bytes 4194320 | tf_op jit(solution)/shard_map/psum | solution.py:148
  874.5 5.4 copy.33
  879.9 56.5 %reduce-scatter.8.cloned.1.call-done = bf16[2048,512]{1,0:T(8,128)(2,1)} async-done(((bf16[2048,1024]{1,0:T(8,128)(2,1)}), bf16[2048,512]{1,0:T(8,128)(2,1)}) %reduce-scatter.8.cloned.1.call-update) | async-done | bytes 2097168 | tf_op jit(solution)/shard_map/reduce_scatter | solution.py:152
  (114 shorter events, 94.3 us)
Async XLA Ops:
  7.2 10.1 %copy-start = (bf16[512,1024]{1,0:T(8,128)(2,1)S(1)}, bf16[512,1024]{1,0:T(8,128)(2,1)}, u32[]{:S(2)}) copy-start(bf16[512,1024]{1,0:T(8,128)(2,1)} %param.22) | copy-start | bytes 3145732
  7.2 10.7 %copy-start.14 = (bf16[128,512]{1,0:T(8,128)(2,1)S(1)}, bf16[128,512]{1,0:T(8,128)(2,1)}, u32[]{:S(2)}) copy-start(bf16[128,512]{1,0:T(8,128)(2,1)} %param.16) | copy-start | bytes 393220
  7.2 16.7 %copy-start.7 = (bf16[1024,512]{1,0:T(8,128)(2,1)S(1)}, bf16[1024,512]{1,0:T(8,128)(2,1)}, u32[]{:S(2)}) copy-start(bf16[1024,512]{1,0:T(8,128)(2,1)} %param.21) | copy-start | bytes 3145732
  7.2 66.5 %all-gather.2.cloned.1.call-start = ((), (), s32[]{:S(2)}) async-start(), calls=%async_computation.3 | async-start | bytes 6291456 | tf_op jit(solution)/shard_map/all_gather | solution.py:82
  7.9 232.3 %reduce-scatter.4.cloned.1.call-start = ((), (), s32[]{:S(2)}) async-start(), calls=%async_computation.4 | async-start | bytes 786432 | tf_op jit(solution)/shard_map/reduce_scatter | solution.py:94
  24.5 66.1 %copy-start.3 = (f32[128,8,64]{0,2,1:T(8,128)}, f32[128,8,64]{0,2,1:T(8,128)S(1)}, u32[]{:S(2)}) copy-start(f32[128,8,64]{0,2,1:T(8,128)S(1)} %bitcast_convert_fusion.3) | copy-start | bytes 786436
  27.5 53.3 %copy-start.9 = (bf16[1024,512]{1,0:T(8,128)(2,1)}, bf16[1024,512]{1,0:T(8,128)(2,1)S(1)}, u32[]{:S(2)}) copy-start(bf16[1024,512]{1,0:T(8,128)(2,1)S(1)} %get-tuple-element.50) | copy-start | bytes 3145732
  73.7 15.8 %copy-start.16 = (s32[16]{0:T(128)S(1)}, s32[16]{0:T(128)}, u32[]{:S(2)}) copy-start(s32[16]{0:T(128)} %param.19) | copy-start | bytes 196
  73.7 18.8 %copy-start.17 = (s32[128]{0:T(128)S(1)}, s32[128]{0:T(128)}, u32[]{:S(2)}) copy-start(s32[128]{0:T(128)} %param.18) | copy-start | bytes 1540
  83.7 9.5 %collective-permute-start = (bf16[128,1024]{0,1:T(8,128)(2,1)}, bf16[128,1024]{0,1:T(8,128)(2,1)S(1)}, u32[]{:S(2)}, u32[]{:S(2)}) collective-permute-start(bf16[128,1024]{0,1:T(8,128)(2,1)} %get-tuple-element.46), channel_id=1, source_target_pairs={{0,2},{2,4},{4,6},{6,8},{8,10},{10,12},{12,14},{14,16},{16,18},{18... | collective-permute-start | bytes 786440 | tf_op jit(solution)/shard_map/ppermute | solution.py:21
  87.5 7.9 collective-permute-start.1
  201.5 17.6 %collective-permute-start.5 = (bf16[128,1024]{1,0:T(8,128)(2,1)}, bf16[128,1024]{1,0:T(8,128)(2,1)}, u32[]{:S(2)}, u32[]{:S(2)}) collective-permute-start(bf16[128,1024]{1,0:T(8,128)(2,1)} %get-tuple-element.38), channel_id=1, source_target_pairs={{2,0},{4,2},{6,4},{8,6},{10,8},{12,10},{14,12},{16,14},{18,16},{20... | collective-permute-start | bytes 786440 | tf_op jit(solution)/shard_map/ppermute | solution.py:32
  203.4 13.7 %collective-permute-start.4 = (bf16[128,1024]{1,0:T(8,128)(2,1)}, bf16[128,1024]{1,0:T(8,128)(2,1)}, u32[]{:S(2)}, u32[]{:S(2)}) collective-permute-start(bf16[128,1024]{1,0:T(8,128)(2,1)} %get-tuple-element.39), channel_id=1, source_target_pairs={{0,2},{2,4},{4,6},{6,8},{8,10},{10,12},{12,14},{14,16},{16,18},{18... | collective-permute-start | bytes 786440 | tf_op jit(solution)/shard_map/ppermute | solution.py:32
  217.1 96.8 %reduce-scatter.6.cloned.1.call-start = ((), (), s32[]{:S(2)}) async-start(), calls=%async_computation.5 | async-start | bytes 393216 | tf_op jit(solution)/shard_map/reduce_scatter | solution.py:110
  221.1 28.3 %copy-start.12 = (bf16[1024,512]{1,0:T(8,128)(2,1)S(1)}, bf16[1024,512]{1,0:T(8,128)(2,1)}, u32[]{:S(2)}) copy-start(bf16[1024,512]{1,0:T(8,128)(2,1)} %get-tuple-element.48) | copy-start | bytes 3145732
  221.1 28.3 %copy-start.13 = (bf16[1024,512]{1,0:T(8,128)(2,1)S(1)}, bf16[1024,512]{1,0:T(8,128)(2,1)}, u32[]{:S(2)}) copy-start(bf16[1024,512]{1,0:T(8,128)(2,1)} %get-tuple-element.49) | copy-start | bytes 3145732
  241.2 72.7 %copy-start.6 = (bf16[128,512]{1,0:T(8,128)(2,1)}, bf16[128,512]{1,0:T(8,128)(2,1)S(1)}, u32[]{:S(2)}) copy-start(bf16[128,512]{1,0:T(8,128)(2,1)S(1)} %add_convert_fusion.1) | copy-start | bytes 393220
  249.9 6.6 collective-permute-start.2
  254.5 5.6 collective-permute-start.3
  274.7 4.7 copy-start.15
  291.1 4.4 copy-start.8
  296.7 577.9 %all-reduce.2.cloned.1.call-start = ((), (), s32[]{:S(2)}) async-start(), calls=%async_computation.7 | async-start | bytes 8388608 | tf_op jit(solution)/shard_map/psum | solution.py:148
  301.6 634.8 %reduce-scatter.8.cloned.1.call-start = ((), (), s32[]{:S(2)}) async-start(), calls=%async_computation.6 | async-start | bytes 6291456 | tf_op jit(solution)/shard_map/reduce_scatter | solution.py:152
  313.9 622.5 %copy-start.1 = (bf16[512,1024]{1,0:T(8,128)(2,1)S(1)}, bf16[512,1024]{1,0:T(8,128)(2,1)}, u32[]{:S(2)}) copy-start(bf16[512,1024]{1,0:T(8,128)(2,1)} %param.22) | copy-start | bytes 3145732
  (5 other events, 11.0 us)
Sparse Core Ops, SparseCore 0:
  9.7 64.0 all-gather.1
  217.2 22.9 reduce-scatter.3
  296.8 17.0 reduce-scatter.5
  316.8 557.6 all-reduce.1
  877.5 58.8 reduce-scatter.7
where the time goes:
time: 945 us; the launch traced here: 943 us
  waiting for transfers between devices  676 us (72%)
  local copies, waits for them, and re-layouts  105 us (11%)
  other arithmetic  76.6 us (8%)
  matrix products  32.9 us (3%)
  blocking collectives  20.2 us (2%)
  starting transfers between devices  18.1 us (2%)
  between operations  14.2 us (2%)
    psum x1, waiting for transfers between devices, shards(): grad_kv = lax.psum(stacked, 'space')  559 us
    reduce_scatter x1, waiting for transfers between devices, shards(): lax.psum_scatter(grid_terms.astype(jnp.bfloat16), 'head', scatter_dimensi...  56.5 us
    all_gather x1, waiting for transfers between devices, shards(): lax.all_gather(grid_feat, 'head', axis=1, tiled=True)  44.6 us
    unnamed x43, local copies, waits for them, and re-layouts  24.8 us
    scatter-add x1, other arithmetic, shards(): jax.ops.segment_sum(edge_grads, wide_index.reshape(m_dev * slots), num_se...  22.8 us
  transfers between devices with their start and end apart: 11, of which 7 were waited for; matrix products, arithmetic and copies ran while one was open for 6% of the time, Pallas kernels for 0%

commit v1 on v0

v1 whole, which is shorter than its diff:
```python
import functools

import jax
import jax.numpy as jnp
from jax import lax
from jax.experimental import pallas as pl
from jax.experimental.pallas import tpu as pltpu
from jax.sharding import PartitionSpec as P

BF = jnp.bfloat16
F32 = jnp.float32
I32 = jnp.int32
MESH = pl.DeviceIdType.MESH

M = 128
K = 16
G = 2048
RIM = 128
WIDE = G + 2 * RIM
R = 32
W = 16
F = 512
HL = 8
SPACE = 64
CHIPS = SPACE // 2
CAP = 3.0
SCALE = 0.125

E1M, E1C, HUP, HDOWN, WY, WFWD, E2, E3, E4, E5, E6, KUP, KDOWN, E8, GUP, GDOWN, PRE, SWAP = range(18)
N_REMOTE = 18


def dot(a, b):
    return jnp.dot(a, b, preferred_element_type=F32)


def dot_t(a, b):
    return lax.dot_general(a, b, (((1,), (1,)), ((), ())), preferred_element_type=F32)


def dot_first(a, b):
    return lax.dot_general(a, b, (((0,), (0,)), ((), ())), preferred_element_type=F32)


def iota(shape, dim):
    return lax.broadcasted_iota(I32, shape, dim)


def body(
    grid_in, mesh_in, src, deg, off, wkv_in, wq_in, wo_in, wm_in, wmo_in, cot_in,
    enc_out, mesh_out, gg_out, gkv_out,
    wide, mf, cf, wkv_own, wkv_oth, wq, wo, wm, wmo, qd, qdt, xs, ut, zy, srow,
    sd, sd_send, sd_recv, pb, att_own, att_send, att_recv, enc_own, enc_send, enc_recv, ef, mkv, mq,
    mo_own, mo_send, mo_recv, mo_val, gedge, halo_send, halo_recv, ggs,
    gb, pre, rsb, fin,
    lsem, osem, ssem, rsem, rs_s, rs_r, ag_s, ag_r, fw_s, fw_r,
):
    s = lax.axis_index("space")
    g = lax.axis_index("head")
    o = 1 - g
    core = s % 2
    chip = s // 2
    sib = s + 1 - 2 * core
    up = (s + 1) % SPACE
    down = (s + SPACE - 1) % SPACE
    ylo = (s // 8) % 2
    across = s + 8 - 16 * ylo
    far = s - 1 + 2 * core
    far = (far + SPACE) % SPACE

    def remote(src_ref, dst_ref, n, dev):
        return pltpu.make_async_remote_copy(
            src_ref=src_ref, dst_ref=dst_ref, send_sem=ssem.at[n], recv_sem=rsem.at[n],
            device_id=dev, device_id_type=MESH,
        )

    partner = (s, o)
    mine = pl.ds(pl.multiple_of(g * F, F), F)
    other = pl.ds(pl.multiple_of(o * F, F), F)

    local = [
        (mesh_in, mf.at[0]),
        (cot_in, cf.at[0]),
        (wq_in.at[mine, :], wq.at[0]),
        (wo_in.at[:, mine], wo.at[0]),
        (wq_in.at[other, :], wq.at[1]),
        (wo_in.at[:, other], wo.at[1]),
        (wkv_in.at[:, mine, :], wkv_own),
        (grid_in, wide.at[pl.ds(RIM, G), :]),
        (wm_in.at[:, mine, :], wm.at[0]),
        (wm_in.at[:, other, :], wm.at[1]),
        (wmo_in.at[:, mine], wmo.at[0]),
        (wmo_in.at[:, other], wmo.at[1]),
    ]
    loads = [pltpu.make_async_copy(a, b, lsem.at[i]) for i, (a, b) in enumerate(local)]
    for c in loads:
        c.start()

    barrier = pltpu.get_barrier_semaphore()
    for dev in (partner, (across, o), (sib, g), (far, g)):
        pl.semaphore_signal(barrier, inc=1, device_id=dev, device_id_type=MESH)

    def greet(i, carry):
        pl.semaphore_signal(
            barrier, inc=1, device_id=(((chip + i) % CHIPS) * 2 + core, g), device_id_type=MESH
        )
        return carry

    lax.fori_loop(1, CHIPS, greet, 0)
    pl.semaphore_wait(barrier, 4 + CHIPS - 1)

    e1m = remote(mesh_in, mf.at[1], E1M, partner)
    e1c = remote(cot_in, cf.at[1], E1C, partner)
    hup = remote(grid_in.at[pl.ds(G - RIM, RIM), :], wide.at[pl.ds(0, RIM), :], HUP, (up, g))
    hdown = remote(grid_in.at[pl.ds(0, RIM), :], wide.at[pl.ds(RIM + G, RIM), :], HDOWN, (down, g))
    wy = remote(wkv_in.at[core, other, :], wkv_oth.at[core], WY, (across, o))
    wfwd = remote(wkv_oth.at[core], wkv_oth.at[core], WFWD, (sib, g))
    e1m.start()
    e1c.start()
    hup.start()
    hdown.start()
    wy.start()

    base = s * G - RIM
    rel = src[...] - base
    rel = jnp.where((rel >= 0) & (rel < WIDE), rel, 4095)
    hi = (rel // 64).astype(F32).astype(BF)
    lo = (rel % 64).astype(F32).astype(BF)
    spread = jnp.where(iota((K, 256), 0) == (iota((K, 256), 1) & 15), 1.0, 0.0).astype(BF)
    flat = dot(hi, spread) * 64.0 + dot(lo, spread)
    flat = jnp.where((iota((M, 256), 0) & 15) == iota((M, 256), 1) // 16, flat, 0.0)
    for t in range(8):
        srow[0:1, t * 256 : (t + 1) * 256] = jnp.sum(
            flat[t * 16 : (t + 1) * 16], axis=0, keepdims=True
        )

    for n in (0, 1, 2, 3):
        loads[n].wait()
    qa = dot(mf[0], wq[0])
    da = dot_t(cf[0], wo[0])
    loads[4].wait()
    loads[5].wait()
    e1m.wait_recv()
    e1c.wait_recv()
    qa = qa + dot(mf[1], wq[1])
    da = da + dot_t(cf[1], wo[1])
    qd[0, 0] = qa.astype(BF)
    qd[0, 1] = da.astype(BF)
    e2 = remote(qd.at[0], qd.at[1], E2, partner)
    e2.start()

    def turn(side):
        for k in range(2):
            qdt[side, k] = qd[side, k].astype(F32).T.astype(BF)

    turn(0)

    def expand(side, weights):
        for k in range(2):
            for a in range(2):
                x4 = qd[side, k, :, a * 256 : (a + 1) * 256].astype(F32)
                head = iota((M, 256), 1) // 64
                lhs = jnp.concatenate(
                    [jnp.where(head == i, x4, 0.0).astype(BF) for i in range(4)], axis=0
                )
                out = dot_t(lhs, weights[k, :, a * 256 : (a + 1) * 256]).astype(BF)
                n = side * HL + a * 4
                ut[k, n : n + 4] = out.reshape(4, M, F)

    loads[6].wait()
    expand(0, wkv_own)

    loads[7].wait()
    hup.wait_recv()
    hdown.wait_recv()

    def gather(t, carry):
        n = pl.multiple_of(t * 32, 32)
        part = (src[pl.ds(n, 32), :] - base).astype(F32)
        part = jnp.broadcast_to(part[:, None, :], (32, K, K)).reshape(512, K)
        pick = (iota((512, K), 0) & 15) == iota((512, K), 1)
        col = jnp.sum(jnp.where(pick, part, 0.0), axis=1, keepdims=True).astype(I32)
        hot = jnp.where(iota((512, WIDE), 1) == col, 1.0, 0.0).astype(BF)
        xs[pl.ds(pl.multiple_of(t * 512, 512), 512), :] = dot(hot, wide[...]).astype(BF)
        return carry

    lax.fori_loop(0, 4, gather, 0)

    wy.wait_recv()
    wfwd.start()
    e2.wait_recv()
    turn(1)
    pltpu.make_async_remote_copy(
        src_ref=wkv_oth.at[1 - core], dst_ref=wkv_oth.at[1 - core], send_sem=ssem.at[WFWD],
        recv_sem=rsem.at[WFWD], device_id=(sib, g), device_id_type=MESH,
    ).wait_recv()
    expand(1, wkv_oth)

    def scores(t, carry):
        xg = xs[pl.ds(pl.multiple_of(t * 256, 256), 256), :]
        lane = iota((K, 256), 1) & 15
        for k in range(2):
            ug = ut[k, :, pl.ds(pl.multiple_of(t * 16, 16), 16), :].reshape(256, F)
            full = dot_t(xg, ug).reshape(16, K, 256)
            total = jnp.zeros((K, 256), F32)
            for m in range(16):
                total = total + jnp.where(lane == m, full[m], 0.0)
            sd[k, t] = total
            sd_send[k, t] = total.astype(BF)
        return carry

    lax.fori_loop(0, 8, scores, 0)
    e3 = remote(sd_send, sd_recv, E3, partner)
    e3.start()

    dg = deg[...].astype(F32)
    dg = jnp.where(iota((8, M), 1) // 16 == iota((8, M), 0), dg, 0.0).astype(BF)
    tile = jnp.where((iota((M, 128), 0) & 15) == (iota((M, 128), 1) & 15), 1.0, 0.0).astype(BF)
    dlane = dot(dg, tile)
    live = iota((8, K, 128), 1).astype(F32) < dlane[:, None, :]

    e3.wait_recv()
    for side in range(2):
        a, b = side * 128, (1 - side) * 128
        raw = (sd[0, :, :, a : a + 128] + sd_recv[0, :, :, b : b + 128].astype(F32)) * SCALE
        dp = sd[1, :, :, a : a + 128] + sd_recv[1, :, :, b : b + 128].astype(F32)
        th = jnp.tanh(raw * (1.0 / CAP))
        wgt = jnp.where(live, jnp.exp(CAP * th), 0.0)
        prob = wgt / jnp.sum(wgt, axis=1, keepdims=True)
        ds = prob * (dp - jnp.sum(prob * dp, axis=1, keepdims=True))
        dr = ds * (1.0 - th * th) * SCALE
        pb[0, :, :, a : a + 128] = prob.astype(BF)
        pb[1, :, :, a : a + 128] = dr.astype(BF)

    def sums(t, carry):
        xg = xs[pl.ds(pl.multiple_of(t * 256, 256), 256), :]
        same = (iota((256, 256), 0) & 15) == iota((256, 256), 1) // 16
        sel = jnp.where(iota((K, 256), 0) == (iota((K, 256), 1) & 15), 1.0, 0.0).astype(BF)
        for k in range(2):
            pt = jnp.where(same, dot_first(pb[k, t], sel), 0.0).astype(BF)
            out = dot(pt, xg).astype(BF)
            zy[k, :, pl.ds(pl.multiple_of(t * 16, 16), 16), :] = out.reshape(16, 16, F)
        return carry

    lax.fori_loop(0, 8, sums, 0)

    def diagonal(x):
        x = x.reshape(4, M, 256)
        head = iota((M, 256), 1) // 64
        out = jnp.zeros((M, 256), F32)
        for i in range(4):
            out = out + jnp.where(head == i, x[i], 0.0)
        return out

    for a in range(2):
        z4 = zy[0, HL + a * 4 : HL + a * 4 + 4].reshape(4 * M, F)
        att_send[:, a * 256 : (a + 1) * 256] = diagonal(
            dot(z4, wkv_oth[1, :, a * 256 : (a + 1) * 256])
        ).astype(BF)
    e4 = remote(att_send, att_recv, E4, partner)
    e4.start()
    for a in range(2):
        z4 = zy[0, a * 4 : a * 4 + 4].reshape(4 * M, F)
        att_own[:, a * 256 : (a + 1) * 256] = diagonal(
            dot(z4, wkv_own[1, :, a * 256 : (a + 1) * 256])
        )

    def weight_terms(n, carry):
        k = (1 - core) + n * (2 * core - 1)
        for side in range(2):
            block0 = (g if side == 0 else o) * 16
            for p in range(4):
                x = qdt[side, k, p * 128 : (p + 1) * 128, :].astype(F32)
                first = iota((128, M), 0) < 64
                lhs = jnp.concatenate(
                    [jnp.where(first, x, 0.0).astype(BF), jnp.where(first, 0.0, x).astype(BF)], axis=1
                )
                h = side * HL + 2 * p
                rhs = zy[1 - k, h : h + 2].reshape(2 * M, F)
                out = dot(lhs, rhs).astype(BF)
                for f in range(4):
                    gb[k, block0 + p * 4 + f] = out[:, f * 128 : (f + 1) * 128]
        return carry

    weight_terms(0, 0)
    presum = remote(gb.at[1 - core], pre, PRE, (sib, g))
    presum.start()
    weight_terms(1, 0)

    e4.wait_recv()
    att = (att_own[...] + att_recv[...].astype(F32)).astype(BF)
    enc_send[...] = dot(att, wo[1]).astype(BF)
    e5 = remote(enc_send, enc_recv, E5, partner)
    e5.start()
    enc_own[...] = dot(att, wo[0])

    presum.wait_recv()

    def scatter_copy(i):
        block = ((chip + i) % CHIPS + 16 * g) % CHIPS
        return pltpu.make_async_remote_copy(
            src_ref=gb.at[core, block], dst_ref=rsb.at[i], send_sem=rs_s.at[i], recv_sem=rs_r.at[i],
            device_id=(((chip + i) % CHIPS) * 2 + core, g), device_id_type=MESH,
        )

    def reduce_send(i, carry):
        block = ((chip + i) % CHIPS + 16 * g) % CHIPS
        gb[core, block] = (gb[core, block].astype(F32) + pre[block].astype(F32)).astype(BF)
        scatter_copy(i).start()
        return carry

    lax.fori_loop(1, CHIPS, reduce_send, 0)

    e5.wait_recv()
    enc = (mf[0].astype(F32) + enc_own[...] + enc_recv[...].astype(F32)).astype(BF)
    ef[0] = enc
    e6 = remote(ef.at[0], ef.at[1], E6, partner)
    e6.start()
    enc_copy = pltpu.make_async_copy(ef.at[0], enc_out, osem.at[0])
    enc_copy.start()

    def edge_grads(t, carry):
        rows = pl.ds(pl.multiple_of(t * 16, 16), 16)
        match = (iota((16, K, 256), 2) & 15) == iota((16, K, 256), 0)
        total = jnp.zeros((256, F), F32)
        for k in range(2):
            p = jnp.broadcast_to(pb[1 - k, t].astype(F32)[None], (16, K, 256))
            p = jnp.where(match, p, 0.0).astype(BF).reshape(256, 256)
            total = total + dot(p, ut[k, :, rows, :].reshape(256, F))
        gedge[pl.ds(pl.multiple_of(t * 256, 256), 256), :] = total.astype(BF)
        return carry

    lax.fori_loop(0, 8, edge_grads, 0)

    loads[8].wait()
    loads[9].wait()
    e6.wait_recv()
    for k in range(2):
        mkv[k, R : R + M, :] = (dot(ef[0], wm[0, 1 + k]) + dot(ef[1], wm[1, 1 + k])).astype(BF)
    kup = remote(mkv.at[:, pl.ds(M, R), :], mkv.at[:, pl.ds(0, R), :], KUP, (up, g))
    kdown = remote(mkv.at[:, pl.ds(R, R), :], mkv.at[:, pl.ds(R + M, R), :], KDOWN, (down, g))
    kup.start()
    kdown.start()
    mq[...] = (dot(ef[0], wm[0, 0]) + dot(ef[1], wm[1, 0])).astype(BF)

    def rows_of(first, count):
        hot = jnp.where(
            (iota((count, G), 0) + first).astype(F32) == srow[0:1, :], 1.0, 0.0
        ).astype(BF)
        return dot(hot, gedge[...])

    halo_send[0] = rows_of(0, RIM).astype(BF)
    halo_send[1] = rows_of(RIM + G, RIM).astype(BF)
    gdown = remote(halo_send.at[0], halo_recv.at[1], GDOWN, (down, g))
    gup = remote(halo_send.at[1], halo_recv.at[0], GUP, (up, g))
    gdown.start()
    gup.start()

    where_n = iota((M, 256), 1) - R
    delta = where_n - iota((M, 256), 0)
    allowed = delta == off[0]
    for j in range(1, W):
        allowed = allowed | (delta == off[j])
    where_g = where_n + s * M
    allowed = allowed & (where_g >= 0) & (where_g < M * SPACE)
    allow = jnp.where(allowed[:, : M + 2 * R], 1.0, 0.0)
    allow4 = jnp.concatenate([allow] * 4, axis=0)
    kup.wait_recv()
    kdown.wait_recv()
    matts = []
    for a in range(2):
        cols = slice(a * 256, (a + 1) * 256)
        x4 = mq[:, cols].astype(F32)
        head = iota((M, 256), 1) // 64
        lhs = jnp.concatenate([jnp.where(head == i, x4, 0.0).astype(BF) for i in range(4)], axis=0)
        raw = dot_t(lhs, mkv[0, :, cols]) * SCALE
        wgt = jnp.exp(CAP * jnp.tanh(raw * (1.0 / CAP))) * allow4
        prob = (wgt / jnp.sum(wgt, axis=1, keepdims=True)).astype(BF)
        matts.append(diagonal(dot(prob, mkv[1, :, cols])).astype(BF))
    matt = jnp.concatenate(matts, axis=1)
    loads[10].wait()
    loads[11].wait()
    mo_send[...] = dot(matt, wmo[1]).astype(BF)
    e8 = remote(mo_send, mo_recv, E8, partner)
    e8.start()
    mo_own[...] = dot(matt, wmo[0])

    own_block = (chip + 16 * g) % CHIPS
    block_sum = gb[core, own_block].astype(F32) + pre[own_block].astype(F32)

    def reduce_recv(i, total):
        scatter_copy(i).wait_recv()
        return total + rsb[i].astype(F32)

    block_sum = lax.fori_loop(1, CHIPS, reduce_recv, block_sum)
    fin[0] = block_sum.T.astype(BF)
    swap = remote(fin.at[0], fin.at[1], SWAP, partner)
    swap.start()

    def interior(t, carry):
        n = pl.multiple_of(t * 512, 512)
        ggs[pl.ds(n, 512), :] = rows_of(n + RIM, 512).astype(BF)
        return carry

    lax.fori_loop(0, 1, interior, 0)

    swap.wait_recv()
    late = chip // 16

    def place(k, c):
        half = g + (c // 16) * (1 - 2 * g)
        row = pl.multiple_of((half * 4 + c % 4) * 128, 128)
        col = pl.multiple_of(((c % 16) // 4) * 128, 128)
        return gkv_out.at[k, pl.ds(row, 128), pl.ds(col, 128)]

    def spread_copy(i, c):
        return pltpu.make_async_remote_copy(
            src_ref=fin.at[late], dst_ref=place(core, c), send_sem=ag_s.at[i], recv_sem=ag_r.at[i],
            device_id=(((chip + i) % CHIPS) * 2 + core, g), device_id_type=MESH,
        )

    def pass_copy(i, k):
        c = (chip + CHIPS - i) % CHIPS
        return pltpu.make_async_remote_copy(
            src_ref=place(k, c), dst_ref=place(k, c), send_sem=fw_s.at[i], recv_sem=fw_r.at[i],
            device_id=(sib, g), device_id_type=MESH,
        )

    def spread_send(i, carry):
        spread_copy(i, chip).start()
        return carry

    lax.fori_loop(1, CHIPS, spread_send, 0)
    own_copy = pltpu.make_async_copy(fin.at[late], place(core, chip), osem.at[1])
    own_copy.start()

    lax.fori_loop(1, 4, interior, 0)
    gdown.wait_recv()
    gup.wait_recv()
    ggs[0:RIM, :] = (ggs[0:RIM, :].astype(F32) + halo_recv[0].astype(F32)).astype(BF)
    ggs[G - RIM : G, :] = (ggs[G - RIM : G, :].astype(F32) + halo_recv[1].astype(F32)).astype(BF)
    gg_copy = pltpu.make_async_copy(ggs, gg_out, osem.at[2])
    gg_copy.start()

    e8.wait_recv()
    mo_val[...] = (ef[0].astype(F32) + mo_own[...] + mo_recv[...].astype(F32)).astype(BF)
    mo_copy = pltpu.make_async_copy(mo_val, mesh_out, osem.at[3])
    mo_copy.start()

    own_copy.wait()
    pass_copy(0, core).start()

    def pass_on(i, carry):
        spread_copy(i, (chip + CHIPS - i) % CHIPS).wait_recv()
        pass_copy(i, core).start()
        return carry

    lax.fori_loop(1, CHIPS, pass_on, 0)

    def finish(i, carry):
        pass_copy(i, 1 - core).wait_recv()
        pass_copy(i, core).wait_send()
        return carry

    lax.fori_loop(0, CHIPS, finish, 0)

    def sent(i, carry):
        scatter_copy(i).wait_send()
        spread_copy(i, chip).wait_send()
        return carry

    lax.fori_loop(1, CHIPS, sent, 0)
    for c in (e1m, e1c, hup, hdown, wy, wfwd, e2, e3, e4, e5, e6, kup, kdown, e8, gdown, gup, presum, swap):
        c.wait_send()
    enc_copy.wait()
    gg_copy.wait()
    mo_copy.wait()


def shards(
    grid_feat, mesh_feat, edge_src, degree, offsets, w_kv, w_query, w_out, w_mesh, w_mesh_out, cotangent
):
    hbm = pl.BlockSpec(memory_space=pl.ANY)
    vmem = pl.BlockSpec(memory_space=pltpu.VMEM)
    smem = pl.BlockSpec(memory_space=pltpu.SMEM)

    def v(*shape, dtype=BF):
        return pltpu.VMEM(shape, dtype)

    dma = pltpu.SemaphoreType.DMA
    scratch = dict(
        wide=v(WIDE, F), mf=v(2, M, F), cf=v(2, M, F), wkv_own=v(2, F, F), wkv_oth=v(2, F, F),
        wq=v(2, F, F), wo=v(2, F, F), wm=v(2, 3, F, F), wmo=v(2, F, F),
        qd=v(2, 2, M, F), qdt=v(2, 2, F, M), xs=v(G, F), ut=v(2, 16, M, F), zy=v(2, 16, M, F),
        srow=v(8, G, dtype=F32),
        sd=v(2, 8, K, 256, dtype=F32), sd_send=v(2, 8, K, 256), sd_recv=v(2, 8, K, 256), pb=v(2, 8, K, 256),
        att_own=v(M, F, dtype=F32), att_send=v(M, F), att_recv=v(M, F),
        enc_own=v(M, F, dtype=F32), enc_send=v(M, F), enc_recv=v(M, F), ef=v(2, M, F),
        mkv=v(2, M + 2 * R, F), mq=v(M, F),
        mo_own=v(M, F, dtype=F32), mo_send=v(M, F), mo_recv=v(M, F), mo_val=v(M, F),
        gedge=v(G, F), halo_send=v(2, RIM, F), halo_recv=v(2, RIM, F), ggs=v(G, F),
        gb=v(2, CHIPS, 128, 128), pre=v(CHIPS, 128, 128), rsb=v(CHIPS, 128, 128), fin=v(2, 128, 128),
        lsem=dma((12,)), osem=dma((4,)), ssem=dma((N_REMOTE,)), rsem=dma((N_REMOTE,)),
        rs_s=dma((CHIPS,)), rs_r=dma((CHIPS,)), ag_s=dma((CHIPS,)), ag_r=dma((CHIPS,)),
        fw_s=dma((CHIPS,)), fw_r=dma((CHIPS,)),
    )
    enc, mesh_out, grad_grid, grad_kv = pl.pallas_call(
        body,
        out_shape=(
            jax.ShapeDtypeStruct((M, F), BF),
            jax.ShapeDtypeStruct((M, F), BF),
            jax.ShapeDtypeStruct((G, F), BF),
            jax.ShapeDtypeStruct((2, 2 * F, F), BF),
        ),
        in_specs=[hbm, hbm, vmem, vmem, smem, hbm, hbm, hbm, hbm, hbm, hbm],
        out_specs=(hbm, hbm, hbm, hbm),
        scratch_shapes=list(scratch.values()),
        compiler_params=pltpu.CompilerParams(
            collective_id=0, has_side_effects=True, vmem_limit_bytes=58 * 2**20
        ),
        name="encoder",
    )(
        grid_feat, mesh_feat, edge_src, degree.reshape(1, M), offsets, w_kv, w_query, w_out, w_mesh,
        w_mesh_out, cotangent,
    )
    return enc, mesh_out, grad_grid, grad_kv.astype(F32)


def solution(mesh):
    in_specs = (
        P("space", "head"),
        P("space", "head"),
        P("space", None),
        P("space"),
        P(),
        P(None, None, "head"),
        P(None, "head"),
        P("head", None),
        P(None, None, "head"),
        P("head", None),
        P("space", "head"),
    )
    out_specs = (P("space", "head"), P("space", "head"), P("space", "head"), P(None, None, "head"))
    return jax.shard_map(shards, mesh=mesh, in_specs=in_specs, out_specs=out_specs, check_vma=False)
```

time: 945 us -> 120 us (0.13)
  waiting for transfers between devices: 676 us -> 0 us
  Pallas kernels: 0 us -> 110 us
  local copies, waits for them, and re-layouts: 105 us -> 4.07 us
  other arithmetic: 76.6 us -> 4.35 us
  matrix products: 32.9 us -> 0 us
  blocking collectives: 20.2 us -> 0 us
  starting transfers between devices: 18.1 us -> 0 us
  between operations: 14.2 us -> 0.67 us
    psum x1 -> x0, waiting for transfers between devices: 559 us -> none  [shards(): grad_kv = lax.psum(stacked, 'space')]
    pallas_call x0 -> x1, Pallas kernels: none -> 110 us  [shards(): pl.pallas_call(body, out_shape=(jax.ShapeDtypeStruct((M, F), BF), jax.Sha...]
    reduce_scatter x3 -> x0, waiting for transfers between devices: 65.6 us -> none  [the longest x1 56.5 us: shards(): lax.psum_scatter(grid_terms.astype(jnp.bfloat16), 'head', scatter_dimensi...]
    all_gather x1 -> x0, waiting for transfers between devices: 44.6 us -> none  [shards(): lax.all_gather(grid_feat, 'head', axis=1, tiled=True)]
    dot_general x9 -> x0, matrix products: 32.9 us -> none  [the longest x1 11.2 us: shards(): lax.dot_general(grid_full, grads_low, (((0,), (0,)), ((), ())), preferred...]
    scatter-add x3 -> x0, other arithmetic: 26.7 us -> none  [the longest x1 22.8 us: shards(): jax.ops.segment_sum(edge_grads, wide_index.reshape(m_dev * slots), num_se...]
    gather x2 -> x0, local copies, waits for them, and re-layouts: 23.7 us -> none  [the longest x1 13.9 us: shards(): kv_wide[wide_index]]
    unnamed x43 -> x10, local copies, waits for them, and re-layouts: 24.8 us -> 4.07 us
  transfers between devices with their start and end apart: 11 -> 0, of which waited for: 7 -> 0; matrix products, arithmetic and copies ran while one was open for 6% -> 0% of each run, Pallas kernels for 0% -> 0%
where the time goes in v1:
time: 120 us; the launch traced here: 119 us
  Pallas kernels  110 us (92%)
  other arithmetic  4.35 us (4%)
  local copies, waits for them, and re-layouts  4.07 us (3%)
    pallas_call x1, Pallas kernels, shards(): pl.pallas_call(body, out_shape=(jax.ShapeDtypeStruct((M, F), BF), jax.Sha...  110 us
    convert_element_type x1, other arithmetic, shards(): return (enc, mesh_out, grad_grid, grad_kv.astype(F32))  4.35 us
    unnamed x10, local copies, waits for them, and re-layouts  4.07 us

profile of v1, /device:TPU:1, one launch (start us, length us, event | category | flops | bytes accessed | tf_op | source)
XLA Modules:
  0.0 119.1 jit_solution(12055970642055745659)
XLA Ops:
  0.6 1.4 %copy.15.src = s32[128,16]{1,0:T(8,128)} copy(s32[128,16]{0,1:T(8,128)} %param.13) | data formatting | bytes 16384 | tf_op args[2]
  2.1 110.1 %encoder.1 = (bf16[128,512]{1,0:T(8,128)(2,1)}, bf16[128,512]{1,0:T(8,128)(2,1)}, bf16[2048,512]{1,0:T(8,128)(2,1)}, bf16[2,1024,512]{2,1,0:T(8,128)(2,1)}) custom-call(bf16[2048,512]{1,0:T(8,128)(2,1)} %grid_in.1, bf16[128,512]{1,0:T(8,128)(2,1)} %mesh_in.1, s32[128,16]{1,0:T(8,128)} %copy.15.src, s32[1,128]{1,0:T(1,128)} %bitcast.1, s32[16]{0:T(128)} %off.1, ...), custom_call_target="tpu_custom_call" | custom-call | tf_op jit(solution)/shard_map/encoder/pallas_call | solution.py:507
  112.1 0.0 copy-start.2
  112.1 0.0 copy-start.1
  112.1 0.0 copy-start
  112.2 4.3 %convert_element_type.3 = f32[2,1024,512]{2,1,0:T(8,128)} convert(bf16[2,1024,512]{2,1,0:T(8,128)(2,1)} %get-tuple-element.11) | non-fusion elementwise | flops 1048576 | bytes 6291456 | tf_op jit(solution)/shard_map/convert_element_type | solution.py:526
  116.5 0.0 copy-done.2
  116.5 0.7 copy.19
  117.2 0.0 copy-done.1
  117.2 0.7 copy.20
  117.8 0.0 copy-done
  117.8 1.3 %copy.21 = bf16[2048,512]{1,0:T(8,128)(2,1)} copy(bf16[2048,512]{1,0:T(8,128)(2,1)S(1)} %copy-done) | data formatting | bytes 4194304
Async XLA Ops:
  112.1 4.4 %copy-start.2 = (bf16[128,512]{1,0:T(8,128)(2,1)S(1)}, bf16[128,512]{1,0:T(8,128)(2,1)}, u32[]{:S(2)}) copy-start(bf16[128,512]{1,0:T(8,128)(2,1)} %get-tuple-element.16) | copy-start | bytes 393220
  112.1 5.0 %copy-start.1 = (bf16[128,512]{1,0:T(8,128)(2,1)S(1)}, bf16[128,512]{1,0:T(8,128)(2,1)}, u32[]{:S(2)}) copy-start(bf16[128,512]{1,0:T(8,128)(2,1)} %get-tuple-element.17) | copy-start | bytes 393220
  112.1 5.7 %copy-start = (bf16[2048,512]{1,0:T(8,128)(2,1)S(1)}, bf16[2048,512]{1,0:T(8,128)(2,1)}, u32[]{:S(2)}) copy-start(bf16[2048,512]{1,0:T(8,128)(2,1)} %get-tuple-element.18) | copy-start | bytes 6291460

commit v2 on v1

--- a/solution.py
+++ b/solution.py
@@ -26,8 +26,11 @@
 CAP = 3.0
 SCALE = 0.125
 
-E1M, E1C, HUP, HDOWN, WY, WFWD, E2, E3, E4, E5, E6, KUP, KDOWN, E8, GUP, GDOWN, PRE, SWAP = range(18)
-N_REMOTE = 18
+(
+    E1M, E1C, HUP, HDOWN, WY, WX, WZ, WXZ, E2, E3, E4, E5, E6, KUP, KDOWN, E8, GUP, GDOWN, AGP,
+    WF, PRE,
+) = list(range(20)) + [23]
+N_REMOTE = 27
 
 
 def dot(a, b):
@@ -49,11 +52,11 @@
 def body(
     grid_in, mesh_in, src, deg, off, wkv_in, wq_in, wo_in, wm_in, wmo_in, cot_in,
     enc_out, mesh_out, gg_out, gkv_out,
-    wide, mf, cf, wkv_own, wkv_oth, wq, wo, wm, wmo, qd, qdt, xs, ut, zy, srow,
+    nodes, wide, mf, cf, wkv_own, wkv_oth, wq, wo, wm, wmo, qd, qdt, xs, ut, zy, srow,
     sd, sd_send, sd_recv, pb, att_own, att_send, att_recv, enc_own, enc_send, enc_recv, ef, mkv, mq,
     mo_own, mo_send, mo_recv, mo_val, gedge, halo_send, halo_recv, ggs,
     gb, pre, rsb, fin,
-    lsem, osem, ssem, rsem, rs_s, rs_r, ag_s, ag_r, fw_s, fw_r,
+    lsem, osem, ssem, rsem, rs_s, rs_r, ag_s, ag_r, fw_s, fw_r, known,
 ):
     s = lax.axis_index("space")
     g = lax.axis_index("head")
@@ -63,8 +66,14 @@
     sib = s + 1 - 2 * core
     up = (s + 1) % SPACE
     down = (s + SPACE - 1) % SPACE
-    ylo = (s // 8) % 2
-    across = s + 8 - 16 * ylo
+
+    def flip(bit):
+        return s + bit - 2 * bit * ((s // bit) % 2)
+
+    across = flip(8)
+    beside_x, beside_z = flip(16), flip(2)
+    beside_xz = beside_x + beside_z - s
+    quarter = (chip // 8 % 2) * 2 + chip % 2
     far = s - 1 + 2 * core
     far = (far + SPACE) % SPACE
 
@@ -96,33 +105,49 @@
     for c in loads:
         c.start()
 
+    bits = [partner, (flip(2), g), (flip(4), g), (flip(8), g), (flip(16), g), (flip(32), g)]
+    first = bits + [(across, o), (sib, g), (far, g), (beside_xz, g)]
     barrier = pltpu.get_barrier_semaphore()
-    for dev in (partner, (across, o), (sib, g), (far, g)):
+    for dev in first:
         pl.semaphore_signal(barrier, inc=1, device_id=dev, device_id_type=MESH)
-
-    def greet(i, carry):
-        pl.semaphore_signal(
-            barrier, inc=1, device_id=(((chip + i) % CHIPS) * 2 + core, g), device_id_type=MESH
-        )
-        return carry
-
-    lax.fori_loop(1, CHIPS, greet, 0)
-    pl.semaphore_wait(barrier, 4 + CHIPS - 1)
+    pl.semaphore_wait(barrier, len(first))
+
+    def tell(b):
+        pl.semaphore_signal(known.at[b], inc=1, device_id=bits[b], device_id_type=MESH)
+
+    def hear(b):
+        pl.semaphore_wait(known.at[b], 1)
 
     e1m = remote(mesh_in, mf.at[1], E1M, partner)
     e1c = remote(cot_in, cf.at[1], E1C, partner)
     hup = remote(grid_in.at[pl.ds(G - RIM, RIM), :], wide.at[pl.ds(0, RIM), :], HUP, (up, g))
     hdown = remote(grid_in.at[pl.ds(0, RIM), :], wide.at[pl.ds(RIM + G, RIM), :], HDOWN, (down, g))
-    wy = remote(wkv_in.at[core, other, :], wkv_oth.at[core], WY, (across, o))
-    wfwd = remote(wkv_oth.at[core], wkv_oth.at[core], WFWD, (sib, g))
+
+    def piece(k, q):
+        return wkv_oth.at[k, pl.ds(pl.multiple_of(q * 128, 128), 128), :]
+
+    other_rows = pl.ds(pl.multiple_of(o * F + quarter * 128, 128), 128)
+    wy = remote(wkv_in.at[core, other_rows, :], piece(core, quarter), WY, (across, o))
+    wx = remote(piece(core, quarter), piece(core, quarter), WX, (beside_x, g))
+    wz = remote(piece(core, quarter), piece(core, quarter), WZ, (beside_z, g))
+    wxz = remote(piece(core, quarter), piece(core, quarter), WXZ, (beside_xz, g))
+    part = [quarter]
+    part.append(quarter + 1 - 2 * (quarter % 2))
+    part.append(quarter + 2 - 4 * (quarter // 2))
+    part.append(part[1] + part[2] - quarter)
+    wfwd = [remote(piece(core, q), piece(core, q), WF + n, (sib, g)) for n, q in enumerate(part)]
+    wback = [remote(piece(1 - core, q), piece(1 - core, q), WF + n, (sib, g)) for n, q in enumerate(part)]
+    wy.start()
     e1m.start()
     e1c.start()
     hup.start()
     hdown.start()
-    wy.start()
+    tell(0)
 
     base = s * G - RIM
-    rel = src[...] - base
+    source = src[...].astype(F32).T.astype(I32)
+    nodes[...] = source
+    rel = source - base
     rel = jnp.where((rel >= 0) & (rel < WIDE), rel, 4095)
     hi = (rel // 64).astype(F32).astype(BF)
     lo = (rel % 64).astype(F32).astype(BF)
@@ -133,6 +158,31 @@
         srow[0:1, t * 256 : (t + 1) * 256] = jnp.sum(
             flat[t * 16 : (t + 1) * 16], axis=0, keepdims=True
         )
+
+    loads[7].wait()
+    hup.wait_recv()
+    hdown.wait_recv()
+
+    def gather(t, carry):
+        n = pl.multiple_of(t * 32, 32)
+        part = (nodes[pl.ds(n, 32), :] - base).astype(F32)
+        part = jnp.broadcast_to(part[:, None, :], (32, K, K)).reshape(512, K)
+        pick = (iota((512, K), 0) & 15) == iota((512, K), 1)
+        col = jnp.sum(jnp.where(pick, part, 0.0), axis=1, keepdims=True).astype(I32)
+        hot = jnp.where(iota((512, WIDE), 1) == col, 1.0, 0.0).astype(BF)
+        xs[pl.ds(pl.multiple_of(t * 512, 512), 512), :] = dot(hot, wide[...]).astype(BF)
+        return carry
+
+
+    lax.fori_loop(0, 2, gather, 0)
+    wy.wait_recv()
+    wx.start()
+    wz.start()
+    wxz.start()
+    wfwd[0].start()
+    hear(0)
+    tell(1)
+    lax.fori_loop(2, 3, gather, 0)
 
     for n in (0, 1, 2, 3):
         loads[n].wait()
@@ -149,6 +199,10 @@
     e2 = remote(qd.at[0], qd.at[1], E2, partner)
     e2.start()
 
+    lax.fori_loop(3, 4, gather, 0)
+    hear(1)
+    tell(2)
+
     def turn(side):
         for k in range(2):
             qdt[side, k] = qd[side, k].astype(F32).T.astype(BF)
@@ -170,31 +224,20 @@
     loads[6].wait()
     expand(0, wkv_own)
 
-    loads[7].wait()
-    hup.wait_recv()
-    hdown.wait_recv()
-
-    def gather(t, carry):
-        n = pl.multiple_of(t * 32, 32)
-        part = (src[pl.ds(n, 32), :] - base).astype(F32)
-        part = jnp.broadcast_to(part[:, None, :], (32, K, K)).reshape(512, K)
-        pick = (iota((512, K), 0) & 15) == iota((512, K), 1)
-        col = jnp.sum(jnp.where(pick, part, 0.0), axis=1, keepdims=True).astype(I32)
-        hot = jnp.where(iota((512, WIDE), 1) == col, 1.0, 0.0).astype(BF)
-        xs[pl.ds(pl.multiple_of(t * 512, 512), 512), :] = dot(hot, wide[...]).astype(BF)
-        return carry
-
-    lax.fori_loop(0, 4, gather, 0)
-
-    wy.wait_recv()
-    wfwd.start()
+    hear(2)
+    tell(3)
+    for n, c in ((1, wz), (2, wx), (3, wxz)):
+        remote(piece(core, part[n]), piece(core, part[n]), (WZ, WX, WXZ)[n - 1], partner).wait_recv()
+        wfwd[n].start()
     e2.wait_recv()
     turn(1)
-    pltpu.make_async_remote_copy(
-        src_ref=wkv_oth.at[1 - core], dst_ref=wkv_oth.at[1 - core], send_sem=ssem.at[WFWD],
-        recv_sem=rsem.at[WFWD], device_id=(sib, g), device_id_type=MESH,
-    ).wait_recv()
+    hear(3)
+    tell(4)
+    for c in wback:
+        c.wait_recv()
     expand(1, wkv_oth)
+    hear(4)
+    tell(5)
 
     def scores(t, carry):
         xg = xs[pl.ds(pl.multiple_of(t * 256, 256), 256), :]
@@ -212,6 +255,8 @@
     lax.fori_loop(0, 8, scores, 0)
     e3 = remote(sd_send, sd_recv, E3, partner)
     e3.start()
+
+    hear(5)
 
     dg = deg[...].astype(F32)
     dg = jnp.where(iota((8, M), 1) // 16 == iota((8, M), 0), dg, 0.0).astype(BF)
@@ -268,7 +313,6 @@
     def weight_terms(n, carry):
         k = (1 - core) + n * (2 * core - 1)
         for side in range(2):
-            block0 = (g if side == 0 else o) * 16
             for p in range(4):
                 x = qdt[side, k, p * 128 : (p + 1) * 128, :].astype(F32)
                 first = iota((128, M), 0) < 64
@@ -279,13 +323,33 @@
                 rhs = zy[1 - k, h : h + 2].reshape(2 * M, F)
                 out = dot(lhs, rhs).astype(BF)
                 for f in range(4):
-                    gb[k, block0 + p * 4 + f] = out[:, f * 128 : (f + 1) * 128]
+                    place_at = (16 * side + 4 * p + f + CHIPS - chip) % CHIPS
+                    gb[k, place_at] = out[:, f * 128 : (f + 1) * 128]
         return carry
 
     weight_terms(0, 0)
-    presum = remote(gb.at[1 - core], pre, PRE, (sib, g))
-    presum.start()
+    presum = [
+        remote(gb.at[1 - core, pl.ds(8 * n, 8)], pre.at[pl.ds(8 * n, 8)], PRE + n, (sib, g))
+        for n in range(4)
+    ]
+    for c in presum:
+        c.start()
     weight_terms(1, 0)
+
+    def scatter_copy(i):
+        return pltpu.make_async_remote_copy(
+            src_ref=gb.at[core, i], dst_ref=rsb.at[i], send_sem=rs_s.at[i], recv_sem=rs_r.at[i],
+            device_id=(((chip + i) % CHIPS) * 2 + core, g), device_id_type=MESH,
+        )
+
+    def reduce_send(i, carry):
+        gb[core, i] = (gb[core, i].astype(F32) + pre[i].astype(F32)).astype(BF)
+        scatter_copy(i).start()
+        return carry
+
+    for n in range(4):
+        presum[n].wait_recv()
+        lax.fori_loop(max(1, 8 * n), 8 * n + 8, reduce_send, 0)
 
     e4.wait_recv()
     att = (att_own[...] + att_recv[...].astype(F32)).astype(BF)
@@ -293,31 +357,6 @@
     e5 = remote(enc_send, enc_recv, E5, partner)
     e5.start()
     enc_own[...] = dot(att, wo[0])
-
-    presum.wait_recv()
-
-    def scatter_copy(i):
-        block = ((chip + i) % CHIPS + 16 * g) % CHIPS
-        return pltpu.make_async_remote_copy(
-            src_ref=gb.at[core, block], dst_ref=rsb.at[i], send_sem=rs_s.at[i], recv_sem=rs_r.at[i],
-            device_id=(((chip + i) % CHIPS) * 2 + core, g), device_id_type=MESH,
-        )
-
-    def reduce_send(i, carry):
-        block = ((chip + i) % CHIPS + 16 * g) % CHIPS
-        gb[core, block] = (gb[core, block].astype(F32) + pre[block].astype(F32)).astype(BF)
-        scatter_copy(i).start()
-        return carry
-
-    lax.fori_loop(1, CHIPS, reduce_send, 0)
-
-    e5.wait_recv()
-    enc = (mf[0].astype(F32) + enc_own[...] + enc_recv[...].astype(F32)).astype(BF)
-    ef[0] = enc
-    e6 = remote(ef.at[0], ef.at[1], E6, partner)
-    e6.start()
-    enc_copy = pltpu.make_async_copy(ef.at[0], enc_out, osem.at[0])
-    enc_copy.start()
 
     def edge_grads(t, carry):
         rows = pl.ds(pl.multiple_of(t * 16, 16), 16)
@@ -331,6 +370,34 @@
         return carry
 
     lax.fori_loop(0, 8, edge_grads, 0)
+
+    def rows_of(first, count):
+        hot = jnp.where(
+            (iota((count, G), 0) + first).astype(F32) == srow[0:1, :], 1.0, 0.0
+        ).astype(BF)
+        return dot(hot, gedge[...])
+
+    halo_send[0] = rows_of(0, RIM).astype(BF)
+    halo_send[1] = rows_of(RIM + G, RIM).astype(BF)
+    gdown = remote(halo_send.at[0], halo_recv.at[1], GDOWN, (down, g))
+    gup = remote(halo_send.at[1], halo_recv.at[0], GUP, (up, g))
+    gdown.start()
+    gup.start()
+
+    e5.wait_recv()
+    enc = (mf[0].astype(F32) + enc_own[...] + enc_recv[...].astype(F32)).astype(BF)
+    ef[0] = enc
+    e6 = remote(ef.at[0], ef.at[1], E6, partner)
+    e6.start()
+    enc_copy = pltpu.make_async_copy(ef.at[0], enc_out, osem.at[0])
+    enc_copy.start()
+
+    def interior(t, carry):
+        n = pl.multiple_of(t * 512, 512)
+        ggs[pl.ds(n, 512), :] = rows_of(n + RIM, 512).astype(BF)
+        return carry
+
+    lax.fori_loop(0, 2, interior, 0)
 
     loads[8].wait()
     loads[9].wait()
@@ -343,18 +410,61 @@
     kdown.start()
     mq[...] = (dot(ef[0], wm[0, 0]) + dot(ef[1], wm[1, 0])).astype(BF)
 
-    def rows_of(first, count):
-        hot = jnp.where(
-            (iota((count, G), 0) + first).astype(F32) == srow[0:1, :], 1.0, 0.0
-        ).astype(BF)
-        return dot(hot, gedge[...])
-
-    halo_send[0] = rows_of(0, RIM).astype(BF)
-    halo_send[1] = rows_of(RIM + G, RIM).astype(BF)
-    gdown = remote(halo_send.at[0], halo_recv.at[1], GDOWN, (down, g))
-    gup = remote(halo_send.at[1], halo_recv.at[0], GUP, (up, g))
-    gdown.start()
-    gup.start()
+    block_sum = gb[core, 0].astype(F32) + pre[0].astype(F32)
+
+    def reduce_recv(i, total):
+        scatter_copy(i).wait_recv()
+        return total + rsb[i].astype(F32)
+
+    block_sum = lax.fori_loop(1, CHIPS, reduce_recv, block_sum)
+    fin[...] = block_sum.T.astype(BF)
+
+    late = chip // 16
+    group = g + late * (1 - 2 * g)
+
+    def place(k, half, c):
+        row = pl.multiple_of((half * 4 + c % 4) * 128, 128)
+        col = pl.multiple_of(((c % 16) // 4) * 128, 128)
+        return gkv_out.at[k, pl.ds(row, 128), pl.ds(col, 128)]
+
+    def spread_copy(i):
+        return pltpu.make_async_remote_copy(
+            src_ref=fin, dst_ref=place(core, g, chip), send_sem=ag_s.at[i], recv_sem=ag_r.at[i],
+            device_id=(((chip + i) % CHIPS) * 2 + core, group), device_id_type=MESH,
+        )
+
+    def arrived(i, k):
+        c = (chip + CHIPS - i) % CHIPS
+        return place(k, g + (c // 16) * (1 - 2 * g), c)
+
+    def spread_recv(i):
+        return pltpu.make_async_remote_copy(
+            src_ref=fin, dst_ref=arrived(i, core), send_sem=ag_s.at[i], recv_sem=ag_r.at[i],
+            device_id=partner, device_id_type=MESH,
+        )
+
+    def pass_copy(i, k):
+        return pltpu.make_async_remote_copy(
+            src_ref=arrived(i, k), dst_ref=arrived(i, k), send_sem=fw_s.at[i], recv_sem=fw_r.at[i],
+            device_id=(sib, g), device_id_type=MESH,
+        )
+
+    own_copy = pltpu.make_async_copy(fin, place(core, g, chip), osem.at[1])
+    own_send = remote(fin, place(core, g, chip), AGP, partner)
+
+    @pl.when(late == 0)
+    def _():
+        own_copy.start()
+
+    @pl.when(late == 1)
+    def _():
+        own_send.start()
+
+    def spread_send(i, carry):
+        spread_copy(i).start()
+        return carry
+
+    lax.fori_loop(1, CHIPS, spread_send, 0)
 
     where_n = iota((M, 256), 1) - R
     delta = where_n - iota((M, 256), 0)
@@ -385,56 +495,7 @@
     e8.start()
     mo_own[...] = dot(matt, wmo[0])
 
-    own_block = (chip + 16 * g) % CHIPS
-    block_sum = gb[core, own_block].astype(F32) + pre[own_block].astype(F32)
-
-    def reduce_recv(i, total):
-        scatter_copy(i).wait_recv()
-        return total + rsb[i].astype(F32)
-
-    block_sum = lax.fori_loop(1, CHIPS, reduce_recv, block_sum)
-    fin[0] = block_sum.T.astype(BF)
-    swap = remote(fin.at[0], fin.at[1], SWAP, partner)
-    swap.start()
-
-    def interior(t, carry):
-        n = pl.multiple_of(t * 512, 512)
-        ggs[pl.ds(n, 512), :] = rows_of(n + RIM, 512).astype(BF)
-        return carry
-
-    lax.fori_loop(0, 1, interior, 0)
-
-    swap.wait_recv()
-    late = chip // 16
-
-    def place(k, c):
-        half = g + (c // 16) * (1 - 2 * g)
-        row = pl.multiple_of((half * 4 + c % 4) * 128, 128)
-        col = pl.multiple_of(((c % 16) // 4) * 128, 128)
-        return gkv_out.at[k, pl.ds(row, 128), pl.ds(col, 128)]
-
-    def spread_copy(i, c):
-        return pltpu.make_async_remote_copy(
-            src_ref=fin.at[late], dst_ref=place(core, c), send_sem=ag_s.at[i], recv_sem=ag_r.at[i],
-            device_id=(((chip + i) % CHIPS) * 2 + core, g), device_id_type=MESH,
-        )
-
-    def pass_copy(i, k):
-        c = (chip + CHIPS - i) % CHIPS
-        return pltpu.make_async_remote_copy(
-            src_ref=place(k, c), dst_ref=place(k, c), send_sem=fw_s.at[i], recv_sem=fw_r.at[i],
-            device_id=(sib, g), device_id_type=MESH,
-        )
-
-    def spread_send(i, carry):
-        spread_copy(i, chip).start()
-        return carry
-
-    lax.fori_loop(1, CHIPS, spread_send, 0)
-    own_copy = pltpu.make_async_copy(fin.at[late], place(core, chip), osem.at[1])
-    own_copy.start()
-
-    lax.fori_loop(1, 4, interior, 0)
+    lax.fori_loop(2, 4, interior, 0)
     gdown.wait_recv()
     gup.wait_recv()
     ggs[0:RIM, :] = (ggs[0:RIM, :].astype(F32) + halo_recv[0].astype(F32)).astype(BF)
@@ -447,11 +508,18 @@
     mo_copy = pltpu.make_async_copy(mo_val, mesh_out, osem.at[3])
     mo_copy.start()
 
-    own_copy.wait()
+    @pl.when(late == 0)
+    def _():
+        own_copy.wait()
+
+    @pl.when(late == 1)
+    def _():
+        remote(fin, arrived(0, core), AGP, partner).wait()
+
     pass_copy(0, core).start()
 
     def pass_on(i, carry):
-        spread_copy(i, (chip + CHIPS - i) % CHIPS).wait_recv()
+        spread_recv(i).wait_recv()
         pass_copy(i, core).start()
         return carry
 
@@ -466,11 +534,12 @@
 
     def sent(i, carry):
         scatter_copy(i).wait_send()
-        spread_copy(i, chip).wait_send()
+        spread_copy(i).wait_send()
         return carry
 
     lax.fori_loop(1, CHIPS, sent, 0)
-    for c in (e1m, e1c, hup, hdown, wy, wfwd, e2, e3, e4, e5, e6, kup, kdown, e8, gdown, gup, presum, swap):
+    singles = [e1m, e1c, hup, hdown, wy, wx, wz, wxz, e2, e3, e4, e5, e6, kup, kdown, e8, gdown, gup]
+    for c in singles + wfwd + presum:
         c.wait_send()
     enc_copy.wait()
     gg_copy.wait()
@@ -489,7 +558,7 @@
 
     dma = pltpu.SemaphoreType.DMA
     scratch = dict(
-        wide=v(WIDE, F), mf=v(2, M, F), cf=v(2, M, F), wkv_own=v(2, F, F), wkv_oth=v(2, F, F),
+        nodes=v(M, K, dtype=I32), wide=v(WIDE, F), mf=v(2, M, F), cf=v(2, M, F), wkv_own=v(2, F, F), wkv_oth=v(2, F, F),
         wq=v(2, F, F), wo=v(2, F, F), wm=v(2, 3, F, F), wmo=v(2, F, F),
         qd=v(2, 2, M, F), qdt=v(2, 2, F, M), xs=v(G, F), ut=v(2, 16, M, F), zy=v(2, 16, M, F),
         srow=v(8, G, dtype=F32),
@@ -499,10 +568,10 @@
         mkv=v(2, M + 2 * R, F), mq=v(M, F),
         mo_own=v(M, F, dtype=F32), mo_send=v(M, F), mo_recv=v(M, F), mo_val=v(M, F),
         gedge=v(G, F), halo_send=v(2, RIM, F), halo_recv=v(2, RIM, F), ggs=v(G, F),
-        gb=v(2, CHIPS, 128, 128), pre=v(CHIPS, 128, 128), rsb=v(CHIPS, 128, 128), fin=v(2, 128, 128),
+        gb=v(2, CHIPS, 128, 128), pre=v(CHIPS, 128, 128), rsb=v(CHIPS, 128, 128), fin=v(128, 128),
         lsem=dma((12,)), osem=dma((4,)), ssem=dma((N_REMOTE,)), rsem=dma((N_REMOTE,)),
         rs_s=dma((CHIPS,)), rs_r=dma((CHIPS,)), ag_s=dma((CHIPS,)), ag_r=dma((CHIPS,)),
-        fw_s=dma((CHIPS,)), fw_r=dma((CHIPS,)),
+        fw_s=dma((CHIPS,)), fw_r=dma((CHIPS,)), known=pltpu.SemaphoreType.REGULAR((6,)),
     )
     enc, mesh_out, grad_grid, grad_kv = pl.pallas_call(
         body,
@@ -520,7 +589,7 @@
         ),
         name="encoder",
     )(
-        grid_feat, mesh_feat, edge_src, degree.reshape(1, M), offsets, w_kv, w_query, w_out, w_mesh,
+        grid_feat, mesh_feat, edge_src.T, degree.reshape(1, M), offsets, w_kv, w_query, w_out, w_mesh,
         w_mesh_out, cotangent,
     )
     return enc, mesh_out, grad_grid, grad_kv.astype(F32)

time: 120 us -> 101 us (0.84)
  the two profiles are of different devices: /device:TPU:1 before, /device:TPU:25 now
where the time goes in v2:
time: 101 us
  Pallas kernels  93.7 us (93%)
  other arithmetic  4.35 us (4%)
  local copies, waits for them, and re-layouts  2.64 us (3%)
    pallas_call x1, Pallas kernels, shards(): pl.pallas_call(body, out_shape=(jax.ShapeDtypeStruct((M, F), BF), jax.Sha...  93.7 us
    convert_element_type x1, other arithmetic, shards(): return (enc, mesh_out, grad_grid, grad_kv.astype(F32))  4.35 us
    unnamed x9, local copies, waits for them, and re-layouts  2.64 us

profile of v2, /device:TPU:25, one launch (start us, length us, event | category | flops | bytes accessed | tf_op | source)
XLA Modules:
  0.0 101.3 jit_solution(8377151724895178909)
XLA Ops:
  0.6 93.7 %encoder.1 = (bf16[128,512]{1,0:T(8,128)(2,1)}, bf16[128,512]{1,0:T(8,128)(2,1)}, bf16[2048,512]{1,0:T(8,128)(2,1)}, bf16[2,1024,512]{2,1,0:T(8,128)(2,1)}) custom-call(bf16[2048,512]{1,0:T(8,128)(2,1)} %grid_in.1, bf16[128,512]{1,0:T(8,128)(2,1)} %mesh_in.1, s32[16,128]{1,0:T(8,128)} %bitcast.2, s32[1,128]{1,0:T(1,128)} %bitcast.3, s32[16]{0:T(128)} %off.1, ...), custom_call_target="tpu_custom_call" | custom-call | tf_op jit(solution)/shard_map/encoder/pallas_call | solution.py:576
  94.3 0.0 copy-start.2
  94.3 0.0 copy-start.1
  94.3 0.0 copy-start
  94.3 4.3 %convert_element_type.3 = f32[2,1024,512]{2,1,0:T(8,128)} convert(bf16[2,1024,512]{2,1,0:T(8,128)(2,1)} %get-tuple-element.11) | non-fusion elementwise | flops 1048576 | bytes 6291456 | tf_op jit(solution)/shard_map/convert_element_type | solution.py:595
  98.7 0.0 copy-done.2
  98.7 0.7 copy.18
  99.4 0.0 copy-done.1
  99.4 0.7 copy.19
  100.0 0.0 copy-done
  100.0 1.3 %copy.20 = bf16[2048,512]{1,0:T(8,128)(2,1)} copy(bf16[2048,512]{1,0:T(8,128)(2,1)S(1)} %copy-done) | data formatting | bytes 4194304
Async XLA Ops:
  94.3 4.4 %copy-start.2 = (bf16[128,512]{1,0:T(8,128)(2,1)S(1)}, bf16[128,512]{1,0:T(8,128)(2,1)}, u32[]{:S(2)}) copy-start(bf16[128,512]{1,0:T(8,128)(2,1)} %get-tuple-element.16) | copy-start | bytes 393220
  94.3 5.0 %copy-start.1 = (bf16[128,512]{1,0:T(8,128)(2,1)S(1)}, bf16[128,512]{1,0:T(8,128)(2,1)}, u32[]{:S(2)}) copy-start(bf16[128,512]{1,0:T(8,128)(2,1)} %get-tuple-element.17) | copy-start | bytes 393220
  94.3 5.7 %copy-start = (bf16[2048,512]{1,0:T(8,128)(2,1)S(1)}, bf16[2048,512]{1,0:T(8,128)(2,1)}, u32[]{:S(2)}) copy-start(bf16[2048,512]{1,0:T(8,128)(2,1)} %get-tuple-element.18) | copy-start | bytes 6291460

commit v3 on v2

--- a/solution.py
+++ b/solution.py
@@ -27,10 +27,10 @@
 SCALE = 0.125
 
 (
-    E1M, E1C, HUP, HDOWN, WY, WX, WZ, WXZ, E2, E3, E4, E5, E6, KUP, KDOWN, E8, GUP, GDOWN, AGP,
-    WF, PRE,
-) = list(range(20)) + [23]
-N_REMOTE = 27
+    E1M, E1C, HUP, HDOWN, E2, E3A, E3B, E4, E5, E6, KUP, KDOWN, E8, GUP, GDOWN, AGP,
+    WY, WR, WF, PRE,
+) = list(range(17)) + [18, 24, 32]
+N_REMOTE = 36
 
 
 def dot(a, b):
@@ -71,9 +71,11 @@
         return s + bit - 2 * bit * ((s // bit) % 2)
 
     across = flip(8)
-    beside_x, beside_z = flip(16), flip(2)
-    beside_xz = beside_x + beside_z - s
-    quarter = (chip // 8 % 2) * 2 + chip % 2
+    at_x, at_z = chip // 8, chip % 4
+
+    def along(axis, d):
+        return (s + 16 * d) % SPACE if axis == 0 else s - 2 * at_z + 2 * ((at_z + d) % 4)
+
     far = s - 1 + 2 * core
     far = (far + SPACE) % SPACE
 
@@ -106,7 +108,7 @@
         c.start()
 
     bits = [partner, (flip(2), g), (flip(4), g), (flip(8), g), (flip(16), g), (flip(32), g)]
-    first = bits + [(across, o), (sib, g), (far, g), (beside_xz, g)]
+    first = bits + [(across, o), (sib, g), (far, g), (flip(16) + flip(32) - s, g), (flip(2) + flip(4) - s, g)]
     barrier = pltpu.get_barrier_semaphore()
     for dev in first:
         pl.semaphore_signal(barrier, inc=1, device_id=dev, device_id_type=MESH)
@@ -123,21 +125,28 @@
     hup = remote(grid_in.at[pl.ds(G - RIM, RIM), :], wide.at[pl.ds(0, RIM), :], HUP, (up, g))
     hdown = remote(grid_in.at[pl.ds(0, RIM), :], wide.at[pl.ds(RIM + G, RIM), :], HDOWN, (down, g))
 
-    def piece(k, q):
-        return wkv_oth.at[k, pl.ds(pl.multiple_of(q * 128, 128), 128), :]
-
-    other_rows = pl.ds(pl.multiple_of(o * F + quarter * 128, 128), 128)
-    wy = remote(wkv_in.at[core, other_rows, :], piece(core, quarter), WY, (across, o))
-    wx = remote(piece(core, quarter), piece(core, quarter), WX, (beside_x, g))
-    wz = remote(piece(core, quarter), piece(core, quarter), WZ, (beside_z, g))
-    wxz = remote(piece(core, quarter), piece(core, quarter), WXZ, (beside_xz, g))
-    part = [quarter]
-    part.append(quarter + 1 - 2 * (quarter % 2))
-    part.append(quarter + 2 - 4 * (quarter // 2))
-    part.append(part[1] + part[2] - quarter)
-    wfwd = [remote(piece(core, q), piece(core, q), WF + n, (sib, g)) for n, q in enumerate(part)]
-    wback = [remote(piece(1 - core, q), piece(1 - core, q), WF + n, (sib, g)) for n, q in enumerate(part)]
-    wy.start()
+    def piece(k, axis, q):
+        return wkv_oth.at[k, pl.ds(pl.multiple_of(axis * 256 + q * 64, 64), 64), :]
+
+    at = (at_x, at_z)
+    wy, wring, wfwd, wback = [], [], [], []
+    for axis in range(2):
+        rows = pl.ds(pl.multiple_of(o * F + axis * 256 + at[axis] * 64, 64), 64)
+        here = piece(core, axis, at[axis])
+        wy.append(remote(wkv_in.at[core, rows, :], here, WY + axis, (across, o)))
+        for d in range(4):
+            q = (at[axis] + 4 - d) % 4
+            if d:
+                n = WR + 3 * axis + d - 1
+                wring.append((
+                    remote(here, here, n, (along(axis, d), g)),
+                    remote(piece(core, axis, q), piece(core, axis, q), n, partner),
+                ))
+            n = WF + 4 * axis + d
+            wfwd.append(remote(piece(core, axis, q), piece(core, axis, q), n, (sib, g)))
+            wback.append(remote(piece(1 - core, axis, q), piece(1 - core, axis, q), n, (sib, g)))
+    for c in wy:
+        c.start()
     e1m.start()
     e1c.start()
     hup.start()
@@ -175,11 +184,12 @@
 
 
     lax.fori_loop(0, 2, gather, 0)
-    wy.wait_recv()
-    wx.start()
-    wz.start()
-    wxz.start()
+    for c in wy:
+        c.wait_recv()
+    for c, _ in wring:
+        c.start()
     wfwd[0].start()
+    wfwd[4].start()
     hear(0)
     tell(1)
     lax.fori_loop(2, 3, gather, 0)
@@ -226,9 +236,29 @@
 
     hear(2)
     tell(3)
-    for n, c in ((1, wz), (2, wx), (3, wxz)):
-        remote(piece(core, part[n]), piece(core, part[n]), (WZ, WX, WXZ)[n - 1], partner).wait_recv()
-        wfwd[n].start()
+
+    def scores(side):
+        def step(t, carry):
+            xg = xs[pl.ds(pl.multiple_of(t * 256, 256), 256), :]
+            lane = iota((K, 256), 1) & 15
+            ug = ut[:, side * HL : side * HL + HL, pl.ds(pl.multiple_of(t * 16, 16), 16), :]
+            full = dot_t(xg, ug.reshape(256, F)).reshape(16, K, 256)
+            total = jnp.where(lane == 0, full[0], 0.0)
+            for m in range(1, 16):
+                total = total + jnp.where(lane == m, full[m], 0.0)
+            sd[side, t] = total
+            sd_send[side, t] = total.astype(BF)
+            return carry
+
+        lax.fori_loop(0, 8, step, 0, unroll=2)
+
+    e3a = remote(sd_send.at[0], sd_recv.at[1], E3A, partner)
+    e3b = remote(sd_send.at[1], sd_recv.at[0], E3B, partner)
+    scores(0)
+    e3a.start()
+    for n, (_, c) in enumerate(wring):
+        c.wait_recv()
+        wfwd[n + 1 + n // 3].start()
     e2.wait_recv()
     turn(1)
     hear(3)
@@ -239,23 +269,8 @@
     hear(4)
     tell(5)
 
-    def scores(t, carry):
-        xg = xs[pl.ds(pl.multiple_of(t * 256, 256), 256), :]
-        lane = iota((K, 256), 1) & 15
-        for k in range(2):
-            ug = ut[k, :, pl.ds(pl.multiple_of(t * 16, 16), 16), :].reshape(256, F)
-            full = dot_t(xg, ug).reshape(16, K, 256)
-            total = jnp.zeros((K, 256), F32)
-            for m in range(16):
-                total = total + jnp.where(lane == m, full[m], 0.0)
-            sd[k, t] = total
-            sd_send[k, t] = total.astype(BF)
-        return carry
-
-    lax.fori_loop(0, 8, scores, 0)
-    e3 = remote(sd_send, sd_recv, E3, partner)
-    e3.start()
-
+    scores(1)
+    e3b.start()
     hear(5)
 
     dg = deg[...].astype(F32)
@@ -264,30 +279,29 @@
     dlane = dot(dg, tile)
     live = iota((8, K, 128), 1).astype(F32) < dlane[:, None, :]
 
-    e3.wait_recv()
-    for side in range(2):
-        a, b = side * 128, (1 - side) * 128
-        raw = (sd[0, :, :, a : a + 128] + sd_recv[0, :, :, b : b + 128].astype(F32)) * SCALE
-        dp = sd[1, :, :, a : a + 128] + sd_recv[1, :, :, b : b + 128].astype(F32)
+    for side in (1, 0):
+        (e3a if side else e3b).wait_recv()
+        raw = (sd[side, :, :, :128] + sd_recv[side, :, :, :128].astype(F32)) * SCALE
+        dp = sd[side, :, :, 128:] + sd_recv[side, :, :, 128:].astype(F32)
         th = jnp.tanh(raw * (1.0 / CAP))
         wgt = jnp.where(live, jnp.exp(CAP * th), 0.0)
         prob = wgt / jnp.sum(wgt, axis=1, keepdims=True)
         ds = prob * (dp - jnp.sum(prob * dp, axis=1, keepdims=True))
         dr = ds * (1.0 - th * th) * SCALE
-        pb[0, :, :, a : a + 128] = prob.astype(BF)
-        pb[1, :, :, a : a + 128] = dr.astype(BF)
+        a = side * 128
+        pb[:, :, a : a + 128] = dr.astype(BF)
+        pb[:, :, 256 + a : 256 + a + 128] = prob.astype(BF)
 
     def sums(t, carry):
         xg = xs[pl.ds(pl.multiple_of(t * 256, 256), 256), :]
-        same = (iota((256, 256), 0) & 15) == iota((256, 256), 1) // 16
+        same = (iota((512, 256), 0) & 15) == iota((512, 256), 1) // 16
         sel = jnp.where(iota((K, 256), 0) == (iota((K, 256), 1) & 15), 1.0, 0.0).astype(BF)
-        for k in range(2):
-            pt = jnp.where(same, dot_first(pb[k, t], sel), 0.0).astype(BF)
-            out = dot(pt, xg).astype(BF)
-            zy[k, :, pl.ds(pl.multiple_of(t * 16, 16), 16), :] = out.reshape(16, 16, F)
-        return carry
-
-    lax.fori_loop(0, 8, sums, 0)
+        pt = jnp.where(same, dot_first(pb[t], sel), 0.0).astype(BF)
+        out = dot(pt, xg).astype(BF)
+        zy[:, :, pl.ds(pl.multiple_of(t * 16, 16), 16), :] = out.reshape(2, 16, 16, F)
+        return carry
+
+    lax.fori_loop(0, 8, sums, 0, unroll=2)
 
     def diagonal(x):
         x = x.reshape(4, M, 256)
@@ -296,19 +310,6 @@
         for i in range(4):
             out = out + jnp.where(head == i, x[i], 0.0)
         return out
-
-    for a in range(2):
-        z4 = zy[0, HL + a * 4 : HL + a * 4 + 4].reshape(4 * M, F)
-        att_send[:, a * 256 : (a + 1) * 256] = diagonal(
-            dot(z4, wkv_oth[1, :, a * 256 : (a + 1) * 256])
-        ).astype(BF)
-    e4 = remote(att_send, att_recv, E4, partner)
-    e4.start()
-    for a in range(2):
-        z4 = zy[0, a * 4 : a * 4 + 4].reshape(4 * M, F)
-        att_own[:, a * 256 : (a + 1) * 256] = diagonal(
-            dot(z4, wkv_own[1, :, a * 256 : (a + 1) * 256])
-        )
 
     def weight_terms(n, carry):
         k = (1 - core) + n * (2 * core - 1)
@@ -320,7 +321,7 @@
                     [jnp.where(first, x, 0.0).astype(BF), jnp.where(first, 0.0, x).astype(BF)], axis=1
                 )
                 h = side * HL + 2 * p
-                rhs = zy[1 - k, h : h + 2].reshape(2 * M, F)
+                rhs = zy[k, h : h + 2].reshape(2 * M, F)
                 out = dot(lhs, rhs).astype(BF)
                 for f in range(4):
                     place_at = (16 * side + 4 * p + f + CHIPS - chip) % CHIPS
@@ -334,7 +335,20 @@
     ]
     for c in presum:
         c.start()
+    for a in range(2):
+        z4 = zy[1, HL + a * 4 : HL + a * 4 + 4].reshape(4 * M, F)
+        att_send[:, a * 256 : (a + 1) * 256] = diagonal(
+            dot(z4, wkv_oth[1, :, a * 256 : (a + 1) * 256])
+        ).astype(BF)
+    e4 = remote(att_send, att_recv, E4, partner)
+    e4.start()
     weight_terms(1, 0)
+    for a in range(2):
+        z4 = zy[1, a * 4 : a * 4 + 4].reshape(4 * M, F)
+        att_own[:, a * 256 : (a + 1) * 256] = diagonal(
+            dot(z4, wkv_own[1, :, a * 256 : (a + 1) * 256])
+        )
+
 
     def scatter_copy(i):
         return pltpu.make_async_remote_copy(
@@ -347,7 +361,7 @@
         scatter_copy(i).start()
         return carry
 
-    for n in range(4):
+    for n in range(2):
         presum[n].wait_recv()
         lax.fori_loop(max(1, 8 * n), 8 * n + 8, reduce_send, 0)
 
@@ -358,18 +372,20 @@
     e5.start()
     enc_own[...] = dot(att, wo[0])
 
+    for n in range(2, 4):
+        presum[n].wait_recv()
+        lax.fori_loop(8 * n, 8 * n + 8, reduce_send, 0)
+
     def edge_grads(t, carry):
         rows = pl.ds(pl.multiple_of(t * 16, 16), 16)
-        match = (iota((16, K, 256), 2) & 15) == iota((16, K, 256), 0)
-        total = jnp.zeros((256, F), F32)
-        for k in range(2):
-            p = jnp.broadcast_to(pb[1 - k, t].astype(F32)[None], (16, K, 256))
-            p = jnp.where(match, p, 0.0).astype(BF).reshape(256, 256)
-            total = total + dot(p, ut[k, :, rows, :].reshape(256, F))
+        match = (iota((16, K, 512), 2) & 15) == iota((16, K, 512), 0)
+        p = jnp.broadcast_to(pb[t].astype(F32)[None], (16, K, 512))
+        p = jnp.where(match, p, 0.0).astype(BF).reshape(256, 512)
+        total = dot(p, ut[:, :, rows, :].reshape(512, F))
         gedge[pl.ds(pl.multiple_of(t * 256, 256), 256), :] = total.astype(BF)
         return carry
 
-    lax.fori_loop(0, 8, edge_grads, 0)
+    lax.fori_loop(0, 8, edge_grads, 0, unroll=2)
 
     def rows_of(first, count):
         hot = jnp.where(
@@ -397,7 +413,7 @@
         ggs[pl.ds(n, 512), :] = rows_of(n + RIM, 512).astype(BF)
         return carry
 
-    lax.fori_loop(0, 2, interior, 0)
+    lax.fori_loop(0, 3, interior, 0)
 
     loads[8].wait()
     loads[9].wait()
@@ -409,6 +425,8 @@
     kup.start()
     kdown.start()
     mq[...] = (dot(ef[0], wm[0, 0]) + dot(ef[1], wm[1, 0])).astype(BF)
+
+    lax.fori_loop(3, 4, interior, 0)
 
     block_sum = gb[core, 0].astype(F32) + pre[0].astype(F32)
 
@@ -495,7 +513,6 @@
     e8.start()
     mo_own[...] = dot(matt, wmo[0])
 
-    lax.fori_loop(2, 4, interior, 0)
     gdown.wait_recv()
     gup.wait_recv()
     ggs[0:RIM, :] = (ggs[0:RIM, :].astype(F32) + halo_recv[0].astype(F32)).astype(BF)
@@ -503,7 +520,15 @@
     gg_copy = pltpu.make_async_copy(ggs, gg_out, osem.at[2])
     gg_copy.start()
 
-    e8.wait_recv()
+    def sent(i, carry):
+        scatter_copy(i).wait_send()
+        return carry
+
+    lax.fori_loop(1, CHIPS, sent, 0)
+    singles = [e1m, e1c, hup, hdown, e2, e3a, e3b, e4, e5, e6, kup, kdown, gdown, gup]
+    for c in singles + wy + [c for c, _ in wring] + wfwd + presum:
+        c.wait_send()
+    e8.wait()
     mo_val[...] = (ef[0].astype(F32) + mo_own[...] + mo_recv[...].astype(F32)).astype(BF)
     mo_copy = pltpu.make_async_copy(mo_val, mesh_out, osem.at[3])
     mo_copy.start()
@@ -519,6 +544,7 @@
     pass_copy(0, core).start()
 
     def pass_on(i, carry):
+        spread_copy(i).wait_send()
         spread_recv(i).wait_recv()
         pass_copy(i, core).start()
         return carry
@@ -532,18 +558,30 @@
 
     lax.fori_loop(0, CHIPS, finish, 0)
 
-    def sent(i, carry):
-        scatter_copy(i).wait_send()
-        spread_copy(i).wait_send()
-        return carry
-
-    lax.fori_loop(1, CHIPS, sent, 0)
-    singles = [e1m, e1c, hup, hdown, wy, wx, wz, wxz, e2, e3, e4, e5, e6, kup, kdown, e8, gdown, gup]
-    for c in singles + wfwd + presum:
-        c.wait_send()
     enc_copy.wait()
     gg_copy.wait()
     mo_copy.wait()
+
+
+def write_results(enc, mesh_o, gg, gkv, enc_out, mesh_out, gg_out, gkv_out, e, m, r, low, wide, s_in, s_out, k_in, k_out):
+    plain = ((enc, e, enc_out), (mesh_o, m, mesh_out), (gg, r, gg_out))
+    parts = [(n // 4, pl.ds(n % 4 * 256, 256)) for n in range(8)]
+    loads = [pltpu.make_async_copy(gkv.at[k, rows], low.at[k, rows], k_in.at[n]) for n, (k, rows) in enumerate(parts)]
+    others = [pltpu.make_async_copy(a, b, s_in.at[n]) for n, (a, b, _) in enumerate(plain)]
+    for c in loads + others:
+        c.start()
+    stores = []
+    for n, (k, rows) in enumerate(parts):
+        loads[n].wait()
+        wide[k, rows] = low[k, rows].astype(F32)
+        stores.append(pltpu.make_async_copy(wide.at[k, rows], gkv_out.at[k, rows], k_out.at[n]))
+        stores[-1].start()
+    for n, (_, b, c) in enumerate(plain):
+        others[n].wait()
+        stores.append(pltpu.make_async_copy(b, c, s_out.at[n]))
+        stores[-1].start()
+    for c in stores:
+        c.wait()
 
 
 def shards(
@@ -562,7 +600,7 @@
         wq=v(2, F, F), wo=v(2, F, F), wm=v(2, 3, F, F), wmo=v(2, F, F),
         qd=v(2, 2, M, F), qdt=v(2, 2, F, M), xs=v(G, F), ut=v(2, 16, M, F), zy=v(2, 16, M, F),
         srow=v(8, G, dtype=F32),
-        sd=v(2, 8, K, 256, dtype=F32), sd_send=v(2, 8, K, 256), sd_recv=v(2, 8, K, 256), pb=v(2, 8, K, 256),
+        sd=v(2, 8, K, 256, dtype=F32), sd_send=v(2, 8, K, 256), sd_recv=v(2, 8, K, 256), pb=v(8, K, 512),
         att_own=v(M, F, dtype=F32), att_send=v(M, F), att_recv=v(M, F),
         enc_own=v(M, F, dtype=F32), enc_send=v(M, F), enc_recv=v(M, F), ef=v(2, M, F),
         mkv=v(2, M + 2 * R, F), mq=v(M, F),
@@ -592,7 +630,24 @@
         grid_feat, mesh_feat, edge_src.T, degree.reshape(1, M), offsets, w_kv, w_query, w_out, w_mesh,
         w_mesh_out, cotangent,
     )
-    return enc, mesh_out, grad_grid, grad_kv.astype(F32)
+    dma = pltpu.SemaphoreType.DMA
+    return pl.pallas_call(
+        write_results,
+        out_shape=(
+            jax.ShapeDtypeStruct((M, F), BF),
+            jax.ShapeDtypeStruct((M, F), BF),
+            jax.ShapeDtypeStruct((G, F), BF),
+            jax.ShapeDtypeStruct((2, 2 * F, F), F32),
+        ),
+        in_specs=[hbm] * 4,
+        out_specs=(hbm,) * 4,
+        scratch_shapes=[
+            v(M, F), v(M, F), v(G, F), v(2, 2 * F, F), v(2, 2 * F, F, dtype=F32),
+            dma((3,)), dma((3,)), dma((8,)), dma((8,)),
+        ],
+        compiler_params=pltpu.CompilerParams(vmem_limit_bytes=24 * 2**20),
+        name="results",
+    )(enc, mesh_out, grad_grid, grad_kv)
 
 
 def solution(mesh):

time: 101 us -> 98.6 us (0.976)
  the two profiles are of different devices: /device:TPU:25 before, /device:TPU:1 now
where the time goes in v3:
time: 98.6 us; the launch traced here: 98.4 us
  Pallas kernels  92.8 us (94%)
  local copies, waits for them, and re-layouts  4.98 us (5%)
    pallas_call x1, Pallas kernels, shards(): pl.pallas_call(body, out_shape=(jax.ShapeDtypeStruct((M, F), BF), jax.Sha...  89.1 us
    unnamed x8, local copies, waits for them, and re-layouts  4.98 us
    pallas_call x1, Pallas kernels, shards(): pl.pallas_call(write_results, out_shape=(jax.ShapeDtypeStruct((M, F), BF)...  3.62 us

profile of v3, /device:TPU:1, one launch (start us, length us, event | category | flops | bytes accessed | tf_op | source)
XLA Modules:
  0.0 98.4 jit_solution(8140286209663629646)
XLA Ops:
  0.6 89.1 %encoder.1 = (bf16[128,512]{1,0:T(8,128)(2,1)}, bf16[128,512]{1,0:T(8,128)(2,1)}, bf16[2048,512]{1,0:T(8,128)(2,1)}, bf16[2,1024,512]{2,1,0:T(8,128)(2,1)}) custom-call(bf16[2048,512]{1,0:T(8,128)(2,1)} %grid_in.1, bf16[128,512]{1,0:T(8,128)(2,1)} %mesh_in.1, s32[16,128]{1,0:T(8,128)} %bitcast.2, s32[1,128]{1,0:T(1,128)} %bitcast.3, s32[16]{0:T(128)} %off.1, ...), custom_call_target="tpu_custom_call" | custom-call | tf_op jit(solution)/shard_map/encoder/pallas_call | solution.py:614
  89.8 0.0 copy-start
  89.8 1.6 %copy-done = bf16[2048,512]{1,0:T(8,128)(2,1)S(1)} copy-done((bf16[2048,512]{1,0:T(8,128)(2,1)S(1)}, bf16[2048,512]{1,0:T(8,128)(2,1)}, u32[]{:S(2)}) %copy-start) | copy-done | bytes 2097176
  91.4 0.0 copy-start.1
  91.4 1.6 %copy-done.1 = bf16[2,1024,512]{2,1,0:T(8,128)(2,1)S(1)} copy-done((bf16[2,1024,512]{2,1,0:T(8,128)(2,1)S(1)}, bf16[2,1024,512]{2,1,0:T(8,128)(2,1)}, u32[]{:S(2)}) %copy-start.1) | copy-done | bytes 2097176
  93.0 0.0 copy-start.2
  93.0 0.9 copy-done.2
  93.9 0.0 copy-start.3
  93.9 0.9 copy-done.3
  94.8 3.6 %results.1 = (bf16[128,512]{1,0:T(8,128)(2,1)}, bf16[128,512]{1,0:T(8,128)(2,1)}, bf16[2048,512]{1,0:T(8,128)(2,1)}, f32[2,1024,512]{2,1,0:T(8,128)}) custom-call(bf16[128,512]{1,0:T(8,128)(2,1)S(1)} %copy-done.2, bf16[128,512]{1,0:T(8,128)(2,1)S(1)} %copy-done.3, bf16[2048,512]{1,0:T(8,128)(2,1)S(1)} %copy-done, bf16[2,1024,512]{2,1,0:T(8,128)(2,1)S(1)} %copy-done.1), custom_call_target="tpu_custom_call" | custom-call | tf_op jit(solution)/shard_map/results/pallas_call | solution.py:634
Async XLA Ops:
  89.8 1.6 %copy-start = (bf16[2048,512]{1,0:T(8,128)(2,1)S(1)}, bf16[2048,512]{1,0:T(8,128)(2,1)}, u32[]{:S(2)}) copy-start(bf16[2048,512]{1,0:T(8,128)(2,1)} %get-tuple-element.10.gg) | copy-start | bytes 6291460
  91.4 1.6 %copy-start.1 = (bf16[2,1024,512]{2,1,0:T(8,128)(2,1)S(1)}, bf16[2,1024,512]{2,1,0:T(8,128)(2,1)}, u32[]{:S(2)}) copy-start(bf16[2,1024,512]{2,1,0:T(8,128)(2,1)} %get-tuple-element.11.gkv) | copy-start | bytes 6291460
  93.0 0.9 copy-start.2
  93.9 0.9 copy-start.3

commit v4 on v3

--- a/solution.py
+++ b/solution.py
@@ -27,7 +27,7 @@
 SCALE = 0.125
 
 (
-    E1M, E1C, HUP, HDOWN, E2, E3A, E3B, E4, E5, E6, KUP, KDOWN, E8, GUP, GDOWN, AGP,
+    E1M, E1C, HUP, HDOWN, E2, E3A, E3B, E4, E5, E6, KUP, KDOWN, E8, GUP, GDOWN, SWAP,
     WY, WR, WF, PRE,
 ) = list(range(17)) + [18, 24, 32]
 N_REMOTE = 36
@@ -147,10 +147,10 @@
             wback.append(remote(piece(1 - core, axis, q), piece(1 - core, axis, q), n, (sib, g)))
     for c in wy:
         c.start()
+    hup.start()
+    hdown.start()
     e1m.start()
     e1c.start()
-    hup.start()
-    hdown.start()
     tell(0)
 
     base = s * G - RIM
@@ -168,6 +168,13 @@
             flat[t * 16 : (t + 1) * 16], axis=0, keepdims=True
         )
 
+    for c in wy:
+        c.wait_recv()
+    for c, _ in wring:
+        c.start()
+    wfwd[0].start()
+    wfwd[4].start()
+
     loads[7].wait()
     hup.wait_recv()
     hdown.wait_recv()
@@ -182,17 +189,9 @@
         xs[pl.ds(pl.multiple_of(t * 512, 512), 512), :] = dot(hot, wide[...]).astype(BF)
         return carry
 
-
-    lax.fori_loop(0, 2, gather, 0)
-    for c in wy:
-        c.wait_recv()
-    for c, _ in wring:
-        c.start()
-    wfwd[0].start()
-    wfwd[4].start()
+    lax.fori_loop(0, 3, gather, 0)
     hear(0)
     tell(1)
-    lax.fori_loop(2, 3, gather, 0)
 
     for n in (0, 1, 2, 3):
         loads[n].wait()
@@ -208,6 +207,9 @@
     qd[0, 1] = da.astype(BF)
     e2 = remote(qd.at[0], qd.at[1], E2, partner)
     e2.start()
+    for n, (_, c) in enumerate(wring):
+        c.wait_recv()
+        wfwd[n + 1 + n // 3].start()
 
     lax.fori_loop(3, 4, gather, 0)
     hear(1)
@@ -256,9 +258,6 @@
     e3b = remote(sd_send.at[1], sd_recv.at[0], E3B, partner)
     scores(0)
     e3a.start()
-    for n, (_, c) in enumerate(wring):
-        c.wait_recv()
-        wfwd[n + 1 + n // 3].start()
     e2.wait_recv()
     turn(1)
     hear(3)
@@ -413,7 +412,49 @@
         ggs[pl.ds(n, 512), :] = rows_of(n + RIM, 512).astype(BF)
         return carry
 
-    lax.fori_loop(0, 3, interior, 0)
+    lax.fori_loop(0, 4, interior, 0)
+
+    block_sum = gb[core, 0].astype(F32) + pre[0].astype(F32)
+
+    def reduce_recv(i, total):
+        scatter_copy(i).wait_recv()
+        return total + rsb[i].astype(F32)
+
+    block_sum = lax.fori_loop(1, CHIPS, reduce_recv, block_sum)
+    fin[0] = block_sum.T.astype(BF)
+
+    late = chip // 16
+    swap = remote(fin.at[0], fin.at[1], SWAP, partner)
+
+    def place(k, c):
+        half = g + (c // 16) * (1 - 2 * g)
+        row = pl.multiple_of((half * 4 + c % 4) * 128, 128)
+        col = pl.multiple_of(((c % 16) // 4) * 128, 128)
+        return gkv_out.at[k, pl.ds(row, 128), pl.ds(col, 128)]
+
+    def spread_copy(i):
+        return pltpu.make_async_remote_copy(
+            src_ref=fin.at[late], dst_ref=place(core, chip), send_sem=ag_s.at[i], recv_sem=ag_r.at[i],
+            device_id=(((chip + i) % CHIPS) * 2 + core, g), device_id_type=MESH,
+        )
+
+    own_copy = pltpu.make_async_copy(fin.at[late], place(core, chip), osem.at[1])
+
+    def spread_all():
+        def step(i, carry):
+            spread_copy(i).start()
+            return carry
+
+        lax.fori_loop(1, CHIPS, step, 0)
+        own_copy.start()
+
+    @pl.when(late == 0)
+    def _():
+        spread_all()
+
+    @pl.when(late == 1)
+    def _():
+        swap.start()
 
     loads[8].wait()
     loads[9].wait()
@@ -426,38 +467,17 @@
     kdown.start()
     mq[...] = (dot(ef[0], wm[0, 0]) + dot(ef[1], wm[1, 0])).astype(BF)
 
-    lax.fori_loop(3, 4, interior, 0)
-
-    block_sum = gb[core, 0].astype(F32) + pre[0].astype(F32)
-
-    def reduce_recv(i, total):
-        scatter_copy(i).wait_recv()
-        return total + rsb[i].astype(F32)
-
-    block_sum = lax.fori_loop(1, CHIPS, reduce_recv, block_sum)
-    fin[...] = block_sum.T.astype(BF)
-
-    late = chip // 16
-    group = g + late * (1 - 2 * g)
-
-    def place(k, half, c):
-        row = pl.multiple_of((half * 4 + c % 4) * 128, 128)
-        col = pl.multiple_of(((c % 16) // 4) * 128, 128)
-        return gkv_out.at[k, pl.ds(row, 128), pl.ds(col, 128)]
-
-    def spread_copy(i):
-        return pltpu.make_async_remote_copy(
-            src_ref=fin, dst_ref=place(core, g, chip), send_sem=ag_s.at[i], recv_sem=ag_r.at[i],
-            device_id=(((chip + i) % CHIPS) * 2 + core, group), device_id_type=MESH,
-        )
+    @pl.when(late == 1)
+    def _():
+        swap.wait()
+        spread_all()
 
     def arrived(i, k):
-        c = (chip + CHIPS - i) % CHIPS
-        return place(k, g + (c // 16) * (1 - 2 * g), c)
+        return place(k, (chip + CHIPS - i) % CHIPS)
 
     def spread_recv(i):
         return pltpu.make_async_remote_copy(
-            src_ref=fin, dst_ref=arrived(i, core), send_sem=ag_s.at[i], recv_sem=ag_r.at[i],
+            src_ref=fin.at[0], dst_ref=arrived(i, core), send_sem=ag_s.at[i], recv_sem=ag_r.at[i],
             device_id=partner, device_id_type=MESH,
         )
 
@@ -466,23 +486,6 @@
             src_ref=arrived(i, k), dst_ref=arrived(i, k), send_sem=fw_s.at[i], recv_sem=fw_r.at[i],
             device_id=(sib, g), device_id_type=MESH,
         )
-
-    own_copy = pltpu.make_async_copy(fin, place(core, g, chip), osem.at[1])
-    own_send = remote(fin, place(core, g, chip), AGP, partner)
-
-    @pl.when(late == 0)
-    def _():
-        own_copy.start()
-
-    @pl.when(late == 1)
-    def _():
-        own_send.start()
-
-    def spread_send(i, carry):
-        spread_copy(i).start()
-        return carry
-
-    lax.fori_loop(1, CHIPS, spread_send, 0)
 
     where_n = iota((M, 256), 1) - R
     delta = where_n - iota((M, 256), 0)
@@ -533,14 +536,7 @@
     mo_copy = pltpu.make_async_copy(mo_val, mesh_out, osem.at[3])
     mo_copy.start()
 
-    @pl.when(late == 0)
-    def _():
-        own_copy.wait()
-
-    @pl.when(late == 1)
-    def _():
-        remote(fin, arrived(0, core), AGP, partner).wait()
-
+    own_copy.wait()
     pass_copy(0, core).start()
 
     def pass_on(i, carry):
@@ -606,7 +602,7 @@
         mkv=v(2, M + 2 * R, F), mq=v(M, F),
         mo_own=v(M, F, dtype=F32), mo_send=v(M, F), mo_recv=v(M, F), mo_val=v(M, F),
         gedge=v(G, F), halo_send=v(2, RIM, F), halo_recv=v(2, RIM, F), ggs=v(G, F),
-        gb=v(2, CHIPS, 128, 128), pre=v(CHIPS, 128, 128), rsb=v(CHIPS, 128, 128), fin=v(128, 128),
+        gb=v(2, CHIPS, 128, 128), pre=v(CHIPS, 128, 128), rsb=v(CHIPS, 128, 128), fin=v(2, 128, 128),
         lsem=dma((12,)), osem=dma((4,)), ssem=dma((N_REMOTE,)), rsem=dma((N_REMOTE,)),
         rs_s=dma((CHIPS,)), rs_r=dma((CHIPS,)), ag_s=dma((CHIPS,)), ag_r=dma((CHIPS,)),
         fw_s=dma((CHIPS,)), fw_r=dma((CHIPS,)), known=pltpu.SemaphoreType.REGULAR((6,)),
@@ -645,7 +641,7 @@
             v(M, F), v(M, F), v(G, F), v(2, 2 * F, F), v(2, 2 * F, F, dtype=F32),
             dma((3,)), dma((3,)), dma((8,)), dma((8,)),
         ],
-        compiler_params=pltpu.CompilerParams(vmem_limit_bytes=24 * 2**20),
+        compiler_params=pltpu.CompilerParams(vmem_limit_bytes=58 * 2**20),
         name="results",
     )(enc, mesh_out, grad_grid, grad_kv)
 

time: 98.6 us -> 96.1 us (0.975); the launches traced: 98.4 us -> 94.6 us
  local copies, waits for them, and re-layouts: 4.98 us -> 0 us
  Pallas kernels: 92.8 us -> 94 us
    unnamed x8 -> x0, local copies, waits for them, and re-layouts: 4.98 us -> none
    pallas_call x1, Pallas kernels: 3.62 us -> 4.67 us  [shards(): pl.pallas_call(write_results, out_shape=(jax.ShapeDtypeStruct((M, F), BF)...]
where the time goes in v4:
time: 96.1 us; the launch traced here: 94.6 us
  Pallas kernels  94 us (98%)
    pallas_call x1, Pallas kernels, shards(): pl.pallas_call(body, out_shape=(jax.ShapeDtypeStruct((M, F), BF), jax.Sha...  89.3 us
    pallas_call x1, Pallas kernels, shards(): pl.pallas_call(write_results, out_shape=(jax.ShapeDtypeStruct((M, F), BF)...  4.67 us

profile of v4, /device:TPU:1, one launch (start us, length us, event | category | flops | bytes accessed | tf_op | source)
XLA Modules:
  0.0 94.6 jit_solution(4451255608085107832)
XLA Ops:
  0.6 89.3 %encoder.1 = (bf16[128,512]{1,0:T(8,128)(2,1)}, bf16[128,512]{1,0:T(8,128)(2,1)}, bf16[2048,512]{1,0:T(8,128)(2,1)}, bf16[2,1024,512]{2,1,0:T(8,128)(2,1)}) custom-call(bf16[2048,512]{1,0:T(8,128)(2,1)} %grid_in.1, bf16[128,512]{1,0:T(8,128)(2,1)} %mesh_in.1, s32[16,128]{1,0:T(8,128)} %bitcast.2, s32[1,128]{1,0:T(1,128)} %bitcast.3, s32[16]{0:T(128)} %off.1, ...), custom_call_target="tpu_custom_call" | custom-call | tf_op jit(solution)/shard_map/encoder/pallas_call | solution.py:610
  89.9 4.7 %results.1 = (bf16[128,512]{1,0:T(8,128)(2,1)}, bf16[128,512]{1,0:T(8,128)(2,1)}, bf16[2048,512]{1,0:T(8,128)(2,1)}, f32[2,1024,512]{2,1,0:T(8,128)}) custom-call(bf16[128,512]{1,0:T(8,128)(2,1)} %get-tuple-element.8.enc, bf16[128,512]{1,0:T(8,128)(2,1)} %get-tuple-element.9.mesh_o, bf16[2048,512]{1,0:T(8,128)(2,1)} %get-tuple-element.10.gg, ...), custom_call_target="tpu_custom_call" | custom-call | tf_op jit(solution)/shard_map/results/pallas_call | solution.py:630

commit v5 on v4

--- a/solution.py
+++ b/solution.py
@@ -27,10 +27,10 @@
 SCALE = 0.125
 
 (
-    E1M, E1C, HUP, HDOWN, E2, E3A, E3B, E4, E5, E6, KUP, KDOWN, E8, GUP, GDOWN, SWAP,
-    WY, WR, WF, PRE,
-) = list(range(17)) + [18, 24, 32]
-N_REMOTE = 36
+    E1M, E1C, HUP, HDOWN, E2, E3A, E3B, E4, E5, E6, KUP, KDOWN, E8, GUP, GDOWN,
+    RS3, RS3P, AG1, WY, WR, WF, PRE, RS1, RS2, AG2, AG3, AGF,
+) = list(range(19)) + [20, 26, 34, 36, 42, 48, 54, 60]
+N_REMOTE = 68
 
 
 def dot(a, b):
@@ -55,8 +55,8 @@
     nodes, wide, mf, cf, wkv_own, wkv_oth, wq, wo, wm, wmo, qd, qdt, xs, ut, zy, srow,
     sd, sd_send, sd_recv, pb, att_own, att_send, att_recv, enc_own, enc_send, enc_recv, ef, mkv, mq,
     mo_own, mo_send, mo_recv, mo_val, gedge, halo_send, halo_recv, ggs,
-    gb, pre, rsb, fin,
-    lsem, osem, ssem, rsem, rs_s, rs_r, ag_s, ag_r, fw_s, fw_r, known,
+    gb, pre, rs1, rsum, rs2, tt, tp, rec, bq, bp, blocks,
+    lsem, osem, ssem, rsem, out_s,
 ):
     s = lax.axis_index("space")
     g = lax.axis_index("head")
@@ -70,6 +70,7 @@
     def flip(bit):
         return s + bit - 2 * bit * ((s // bit) % 2)
 
+    ylo = (s // 8) % 2
     across = flip(8)
     at_x, at_z = chip // 8, chip % 4
 
@@ -107,18 +108,12 @@
     for c in loads:
         c.start()
 
-    bits = [partner, (flip(2), g), (flip(4), g), (flip(8), g), (flip(16), g), (flip(32), g)]
-    first = bits + [(across, o), (sib, g), (far, g), (flip(16) + flip(32) - s, g), (flip(2) + flip(4) - s, g)]
+    first = [partner, (across, o), (across, g), (sib, g), (far, g)]
+    first += [(along(axis, d), g) for axis in range(2) for d in (1, 2, 3)]
     barrier = pltpu.get_barrier_semaphore()
     for dev in first:
         pl.semaphore_signal(barrier, inc=1, device_id=dev, device_id_type=MESH)
     pl.semaphore_wait(barrier, len(first))
-
-    def tell(b):
-        pl.semaphore_signal(known.at[b], inc=1, device_id=bits[b], device_id_type=MESH)
-
-    def hear(b):
-        pl.semaphore_wait(known.at[b], 1)
 
     e1m = remote(mesh_in, mf.at[1], E1M, partner)
     e1c = remote(cot_in, cf.at[1], E1C, partner)
@@ -151,7 +146,6 @@
     hdown.start()
     e1m.start()
     e1c.start()
-    tell(0)
 
     base = s * G - RIM
     source = src[...].astype(F32).T.astype(I32)
@@ -190,8 +184,6 @@
         return carry
 
     lax.fori_loop(0, 3, gather, 0)
-    hear(0)
-    tell(1)
 
     for n in (0, 1, 2, 3):
         loads[n].wait()
@@ -212,8 +204,6 @@
         wfwd[n + 1 + n // 3].start()
 
     lax.fori_loop(3, 4, gather, 0)
-    hear(1)
-    tell(2)
 
     def turn(side):
         for k in range(2):
@@ -236,8 +226,6 @@
     loads[6].wait()
     expand(0, wkv_own)
 
-    hear(2)
-    tell(3)
 
     def scores(side):
         def step(t, carry):
@@ -260,17 +248,12 @@
     e3a.start()
     e2.wait_recv()
     turn(1)
-    hear(3)
-    tell(4)
     for c in wback:
         c.wait_recv()
     expand(1, wkv_oth)
-    hear(4)
-    tell(5)
 
     scores(1)
     e3b.start()
-    hear(5)
 
     dg = deg[...].astype(F32)
     dg = jnp.where(iota((8, M), 1) // 16 == iota((8, M), 0), dg, 0.0).astype(BF)
@@ -314,23 +297,24 @@
         k = (1 - core) + n * (2 * core - 1)
         for side in range(2):
             for p in range(4):
-                x = qdt[side, k, p * 128 : (p + 1) * 128, :].astype(F32)
+                xt = qdt[side, k, p * 128 : (p + 1) * 128, :].astype(F32)
                 first = iota((128, M), 0) < 64
                 lhs = jnp.concatenate(
-                    [jnp.where(first, x, 0.0).astype(BF), jnp.where(first, 0.0, x).astype(BF)], axis=1
+                    [jnp.where(first, xt, 0.0).astype(BF), jnp.where(first, 0.0, xt).astype(BF)], axis=1
                 )
                 h = side * HL + 2 * p
                 rhs = zy[k, h : h + 2].reshape(2 * M, F)
                 out = dot(lhs, rhs).astype(BF)
                 for f in range(4):
-                    place_at = (16 * side + 4 * p + f + CHIPS - chip) % CHIPS
-                    gb[k, place_at] = out[:, f * 128 : (f + 1) * 128]
+                    x, y = 2 * side + p // 2, p % 2
+                    gb[k, 0, f, 2 * x + y] = out[:64, f * 128 : (f + 1) * 128]
+                    gb[k, 1, x, 2 * f + y] = out[64:, f * 128 : (f + 1) * 128]
         return carry
 
     weight_terms(0, 0)
     presum = [
-        remote(gb.at[1 - core, pl.ds(8 * n, 8)], pre.at[pl.ds(8 * n, 8)], PRE + n, (sib, g))
-        for n in range(4)
+        remote(gb.at[1 - core, n], pre.at[n], PRE + n, (sib, g))
+        for n in range(2)
     ]
     for c in presum:
         c.start()
@@ -349,20 +333,26 @@
         )
 
 
-    def scatter_copy(i):
-        return pltpu.make_async_remote_copy(
-            src_ref=gb.at[core, i], dst_ref=rsb.at[i], send_sem=rs_s.at[i], recv_sem=rs_r.at[i],
-            device_id=(((chip + i) % CHIPS) * 2 + core, g), device_id_type=MESH,
-        )
-
-    def reduce_send(i, carry):
-        gb[core, i] = (gb[core, i].astype(F32) + pre[i].astype(F32)).astype(BF)
-        scatter_copy(i).start()
-        return carry
-
-    for n in range(2):
-        presum[n].wait_recv()
-        lax.fori_loop(max(1, 8 * n), 8 * n + 8, reduce_send, 0)
+    line = (at_z, at_x)
+    axis_of = (1, 0)
+
+    def ring(h, stage, d):
+        return (along(axis_of[h] if stage == 1 else 1 - axis_of[h], d), g)
+
+    def ahead(n, d):
+        return (n + d) % 4
+
+    stage1 = [
+        remote(gb.at[core, h, ahead(line[h], d)], rs1.at[h, d - 1], RS1 + 3 * h + d - 1, ring(h, 1, d))
+        for h in range(2)
+        for d in (1, 2, 3)
+    ]
+    for h in range(2):
+        presum[h].wait_recv()
+        for n in range(4):
+            gb[core, h, n] = (gb[core, h, n].astype(F32) + pre[h, n].astype(F32)).astype(BF)
+        for c in stage1[3 * h : 3 * h + 3]:
+            c.start()
 
     e4.wait_recv()
     att = (att_own[...] + att_recv[...].astype(F32)).astype(BF)
@@ -370,10 +360,6 @@
     e5 = remote(enc_send, enc_recv, E5, partner)
     e5.start()
     enc_own[...] = dot(att, wo[0])
-
-    for n in range(2, 4):
-        presum[n].wait_recv()
-        lax.fori_loop(8 * n, 8 * n + 8, reduce_send, 0)
 
     def edge_grads(t, carry):
         rows = pl.ds(pl.multiple_of(t * 16, 16), 16)
@@ -386,19 +372,6 @@
 
     lax.fori_loop(0, 8, edge_grads, 0, unroll=2)
 
-    def rows_of(first, count):
-        hot = jnp.where(
-            (iota((count, G), 0) + first).astype(F32) == srow[0:1, :], 1.0, 0.0
-        ).astype(BF)
-        return dot(hot, gedge[...])
-
-    halo_send[0] = rows_of(0, RIM).astype(BF)
-    halo_send[1] = rows_of(RIM + G, RIM).astype(BF)
-    gdown = remote(halo_send.at[0], halo_recv.at[1], GDOWN, (down, g))
-    gup = remote(halo_send.at[1], halo_recv.at[0], GUP, (up, g))
-    gdown.start()
-    gup.start()
-
     e5.wait_recv()
     enc = (mf[0].astype(F32) + enc_own[...] + enc_recv[...].astype(F32)).astype(BF)
     ef[0] = enc
@@ -407,54 +380,59 @@
     enc_copy = pltpu.make_async_copy(ef.at[0], enc_out, osem.at[0])
     enc_copy.start()
 
+    def rows_of(first, count):
+        hot = jnp.where(
+            (iota((count, G), 0) + first).astype(F32) == srow[0:1, :], 1.0, 0.0
+        ).astype(BF)
+        return dot(hot, gedge[...])
+
+    halo_send[0] = rows_of(0, RIM).astype(BF)
+    halo_send[1] = rows_of(RIM + G, RIM).astype(BF)
+    gdown = remote(halo_send.at[0], halo_recv.at[1], GDOWN, (down, g))
+    gup = remote(halo_send.at[1], halo_recv.at[0], GUP, (up, g))
+    gdown.start()
+    gup.start()
+
+    stage2 = [
+        remote(
+            rsum.at[h, pl.ds(2 * ahead(line[1 - h], d), 2)], rs2.at[h, d - 1], RS2 + 3 * h + d - 1, ring(h, 2, d)
+        )
+        for h in range(2)
+        for d in (1, 2, 3)
+    ]
+    for h in range(2):
+        for d in range(3):
+            stage1[3 * h + d].wait_recv()
+        total = gb[core, h, line[h]].astype(F32)
+        for d in range(3):
+            total = total + rs1[h, d].astype(F32)
+        rsum[h] = total.astype(BF)
+        for c in stage2[3 * h : 3 * h + 3]:
+            c.start()
+
     def interior(t, carry):
         n = pl.multiple_of(t * 512, 512)
         ggs[pl.ds(n, 512), :] = rows_of(n + RIM, 512).astype(BF)
         return carry
 
-    lax.fori_loop(0, 4, interior, 0)
-
-    block_sum = gb[core, 0].astype(F32) + pre[0].astype(F32)
-
-    def reduce_recv(i, total):
-        scatter_copy(i).wait_recv()
-        return total + rsb[i].astype(F32)
-
-    block_sum = lax.fori_loop(1, CHIPS, reduce_recv, block_sum)
-    fin[0] = block_sum.T.astype(BF)
-
-    late = chip // 16
-    swap = remote(fin.at[0], fin.at[1], SWAP, partner)
-
-    def place(k, c):
-        half = g + (c // 16) * (1 - 2 * g)
-        row = pl.multiple_of((half * 4 + c % 4) * 128, 128)
-        col = pl.multiple_of(((c % 16) // 4) * 128, 128)
-        return gkv_out.at[k, pl.ds(row, 128), pl.ds(col, 128)]
-
-    def spread_copy(i):
-        return pltpu.make_async_remote_copy(
-            src_ref=fin.at[late], dst_ref=place(core, chip), send_sem=ag_s.at[i], recv_sem=ag_r.at[i],
-            device_id=(((chip + i) % CHIPS) * 2 + core, g), device_id_type=MESH,
-        )
-
-    own_copy = pltpu.make_async_copy(fin.at[late], place(core, chip), osem.at[1])
-
-    def spread_all():
-        def step(i, carry):
-            spread_copy(i).start()
-            return carry
-
-        lax.fori_loop(1, CHIPS, step, 0)
-        own_copy.start()
-
-    @pl.when(late == 0)
-    def _():
-        spread_all()
+    lax.fori_loop(0, 2, interior, 0)
+
+    late = at_x // 2
+    for h in range(2):
+        for d in range(3):
+            stage2[3 * h + d].wait_recv()
+        total = rsum[h, pl.ds(2 * line[1 - h], 2)].astype(F32)
+        for d in range(3):
+            total = total + rs2[h, d].astype(F32)
+        for y in range(2):
+            tt[y, h] = total[y].astype(BF)
+    stage3 = remote(tt.at[1 - ylo], rec, RS3, (across, g + late * (1 - 2 * g)))
+    stage3p = remote(tt.at[ylo], tp, RS3P, partner)
+    stage3.start()
 
     @pl.when(late == 1)
     def _():
-        swap.start()
+        stage3p.start()
 
     loads[8].wait()
     loads[9].wait()
@@ -467,25 +445,38 @@
     kdown.start()
     mq[...] = (dot(ef[0], wm[0, 0]) + dot(ef[1], wm[1, 0])).astype(BF)
 
+    stage3.wait_recv()
+
+    @pl.when(late == 0)
+    def _():
+        tp[...] = tt[ylo]
+
     @pl.when(late == 1)
     def _():
-        swap.wait()
-        spread_all()
-
-    def arrived(i, k):
-        return place(k, (chip + CHIPS - i) % CHIPS)
-
-    def spread_recv(i):
-        return pltpu.make_async_remote_copy(
-            src_ref=fin.at[0], dst_ref=arrived(i, core), send_sem=ag_s.at[i], recv_sem=ag_r.at[i],
-            device_id=partner, device_id_type=MESH,
-        )
-
-    def pass_copy(i, k):
-        return pltpu.make_async_remote_copy(
-            src_ref=arrived(i, k), dst_ref=arrived(i, k), send_sem=fw_s.at[i], recv_sem=fw_r.at[i],
-            device_id=(sib, g), device_id_type=MESH,
-        )
+        stage3p.wait()
+
+    block = (tp[...].astype(F32) + rec[...].astype(F32)).reshape(128, 128).T.astype(BF)
+
+    bq[0, ylo] = block[:64]
+    bq[1, ylo] = block[64:]
+    back1 = remote(bq.at[:, ylo], bq.at[:, ylo], AG1, (across, g))
+    back1.start()
+    lax.fori_loop(2, 3, interior, 0)
+    remote(bq.at[:, 1 - ylo], bq.at[:, 1 - ylo], AG1, (across, g)).wait_recv()
+
+    back2, back2_in, back3, back3_in = [], [], [], []
+    for h in range(2):
+        for d in (1, 2, 3):
+            n = 3 * h + d - 1
+            from2, from3 = ahead(line[1 - h], 4 - d), ahead(line[h], 4 - d)
+            back2.append(remote(bq.at[h], bp.at[h, line[1 - h]], AG2 + n, ring(h, 2, d)))
+            back2_in.append(remote(bq.at[h], bp.at[h, from2], AG2 + n, partner))
+            back3.append(remote(bp.at[h], blocks.at[core, h, line[h]], AG3 + n, ring(h, 1, d)))
+            back3_in.append(remote(bp.at[h], blocks.at[core, h, from3], AG3 + n, partner))
+    for c in back2:
+        c.start()
+    for h in range(2):
+        bp[h, line[1 - h]] = bq[h]
 
     where_n = iota((M, 256), 1) - R
     delta = where_n - iota((M, 256), 0)
@@ -516,6 +507,30 @@
     e8.start()
     mo_own[...] = dot(matt, wmo[0])
 
+    for h in range(2):
+        for c in back2_in[3 * h : 3 * h + 3]:
+            c.wait_recv()
+        for c in back3[3 * h : 3 * h + 3]:
+            c.start()
+        blocks[core, h, line[h]] = bp[h]
+
+    def pass_copy(k, h, d):
+        part = blocks.at[k, h, ahead(line[h], 4 - d)]
+        return remote(part, part, AGF + 4 * h + d, (sib, g))
+
+    def result_copy(k, h, d):
+        n = ahead(line[h], 4 - d)
+        return pltpu.make_async_copy(blocks.at[k, h, n], gkv_out.at[k, h, n], out_s.at[k, 4 * h + d])
+
+    passed = [pass_copy(core, h, d) for h in range(2) for d in range(4)]
+    handed = [pass_copy(1 - core, h, d) for h in range(2) for d in range(4)]
+    mine_out = [result_copy(core, h, d) for h in range(2) for d in range(4)]
+    other_out = [result_copy(1 - core, h, d) for h in range(2) for d in range(4)]
+    for n in (0, 4):
+        passed[n].start()
+        mine_out[n].start()
+
+    lax.fori_loop(3, 4, interior, 0)
     gdown.wait_recv()
     gup.wait_recv()
     ggs[0:RIM, :] = (ggs[0:RIM, :].astype(F32) + halo_recv[0].astype(F32)).astype(BF)
@@ -523,55 +538,57 @@
     gg_copy = pltpu.make_async_copy(ggs, gg_out, osem.at[2])
     gg_copy.start()
 
-    def sent(i, carry):
-        scatter_copy(i).wait_send()
-        return carry
-
-    lax.fori_loop(1, CHIPS, sent, 0)
-    singles = [e1m, e1c, hup, hdown, e2, e3a, e3b, e4, e5, e6, kup, kdown, gdown, gup]
-    for c in singles + wy + [c for c, _ in wring] + wfwd + presum:
+    singles = [e1m, e1c, hup, hdown, e2, e3a, e3b, e4, e5, e6, kup, kdown, gdown, gup, stage3, back1]
+    for c in singles + wy + [c for c, _ in wring] + wfwd + presum + stage1 + stage2 + back2:
         c.wait_send()
     e8.wait()
     mo_val[...] = (ef[0].astype(F32) + mo_own[...] + mo_recv[...].astype(F32)).astype(BF)
     mo_copy = pltpu.make_async_copy(mo_val, mesh_out, osem.at[3])
     mo_copy.start()
 
-    own_copy.wait()
-    pass_copy(0, core).start()
-
-    def pass_on(i, carry):
-        spread_copy(i).wait_send()
-        spread_recv(i).wait_recv()
-        pass_copy(i, core).start()
-        return carry
-
-    lax.fori_loop(1, CHIPS, pass_on, 0)
-
-    def finish(i, carry):
-        pass_copy(i, 1 - core).wait_recv()
-        pass_copy(i, core).wait_send()
-        return carry
-
-    lax.fori_loop(0, CHIPS, finish, 0)
-
+    for d in (1, 2, 3):
+        for h in range(2):
+            back3_in[3 * h + d - 1].wait_recv()
+            passed[4 * h + d].start()
+            mine_out[4 * h + d].start()
+    for c in back3:
+        c.wait_send()
+    for d in range(4):
+        for h in range(2):
+            handed[4 * h + d].wait_recv()
+            other_out[4 * h + d].start()
+    for c in passed:
+        c.wait_send()
     enc_copy.wait()
     gg_copy.wait()
     mo_copy.wait()
+    for c in mine_out + other_out:
+        c.wait()
 
 
 def write_results(enc, mesh_o, gg, gkv, enc_out, mesh_out, gg_out, gkv_out, e, m, r, low, wide, s_in, s_out, k_in, k_out):
     plain = ((enc, e, enc_out), (mesh_o, m, mesh_out), (gg, r, gg_out))
-    parts = [(n // 4, pl.ds(n % 4 * 256, 256)) for n in range(8)]
-    loads = [pltpu.make_async_copy(gkv.at[k, rows], low.at[k, rows], k_in.at[n]) for n, (k, rows) in enumerate(parts)]
+    g = lax.axis_index("head")
+    loads = [pltpu.make_async_copy(gkv.at[k], low.at[k], k_in.at[k]) for k in range(2)]
     others = [pltpu.make_async_copy(a, b, s_in.at[n]) for n, (a, b, _) in enumerate(plain)]
     for c in loads + others:
         c.start()
     stores = []
-    for n, (k, rows) in enumerate(parts):
-        loads[n].wait()
-        wide[k, rows] = low[k, rows].astype(F32)
-        stores.append(pltpu.make_async_copy(wide.at[k, rows], gkv_out.at[k, rows], k_out.at[n]))
-        stores[-1].start()
+    for k in range(2):
+        loads[k].wait()
+        for n in range(2):
+            half = g if n == 0 else 1 - g
+            for x in (2 * n, 2 * n + 1):
+                for z in range(4):
+                    for y in range(2):
+                        col = (x % 2 * 2 + y) * 128
+                        for h in range(2):
+                            rows = pl.ds(pl.multiple_of(half * F + z * 128 + h * 64, 64), 64)
+                            part = low[k, 0, z, x, y] if h == 0 else low[k, 1, x, z, y]
+                            wide[k, rows, col : col + 128] = part.astype(F32)
+            rows = pl.ds(pl.multiple_of(half * F, F), F)
+            stores.append(pltpu.make_async_copy(wide.at[k, rows], gkv_out.at[k, rows], k_out.at[2 * k + n]))
+            stores[-1].start()
     for n, (_, b, c) in enumerate(plain):
         others[n].wait()
         stores.append(pltpu.make_async_copy(b, c, s_out.at[n]))
@@ -602,10 +619,11 @@
         mkv=v(2, M + 2 * R, F), mq=v(M, F),
         mo_own=v(M, F, dtype=F32), mo_send=v(M, F), mo_recv=v(M, F), mo_val=v(M, F),
         gedge=v(G, F), halo_send=v(2, RIM, F), halo_recv=v(2, RIM, F), ggs=v(G, F),
-        gb=v(2, CHIPS, 128, 128), pre=v(CHIPS, 128, 128), rsb=v(CHIPS, 128, 128), fin=v(2, 128, 128),
+        gb=v(2, 2, 4, 8, 64, 128), pre=v(2, 4, 8, 64, 128), rs1=v(2, 3, 8, 64, 128), rsum=v(2, 8, 64, 128),
+        rs2=v(2, 3, 2, 64, 128), tt=v(2, 2, 64, 128), tp=v(2, 64, 128), rec=v(2, 64, 128),
+        bq=v(2, 2, 64, 128), bp=v(2, 4, 2, 64, 128), blocks=v(2, 2, 4, 4, 2, 64, 128),
         lsem=dma((12,)), osem=dma((4,)), ssem=dma((N_REMOTE,)), rsem=dma((N_REMOTE,)),
-        rs_s=dma((CHIPS,)), rs_r=dma((CHIPS,)), ag_s=dma((CHIPS,)), ag_r=dma((CHIPS,)),
-        fw_s=dma((CHIPS,)), fw_r=dma((CHIPS,)), known=pltpu.SemaphoreType.REGULAR((6,)),
+        out_s=dma((2, 8)),
     )
     enc, mesh_out, grad_grid, grad_kv = pl.pallas_call(
         body,
@@ -613,7 +631,7 @@
             jax.ShapeDtypeStruct((M, F), BF),
             jax.ShapeDtypeStruct((M, F), BF),
             jax.ShapeDtypeStruct((G, F), BF),
-            jax.ShapeDtypeStruct((2, 2 * F, F), BF),
+            jax.ShapeDtypeStruct((2, 2, 4, 4, 2, 64, 128), BF),
         ),
         in_specs=[hbm, hbm, vmem, vmem, smem, hbm, hbm, hbm, hbm, hbm, hbm],
         out_specs=(hbm, hbm, hbm, hbm),
@@ -638,8 +656,8 @@
         in_specs=[hbm] * 4,
         out_specs=(hbm,) * 4,
         scratch_shapes=[
-            v(M, F), v(M, F), v(G, F), v(2, 2 * F, F), v(2, 2 * F, F, dtype=F32),
-            dma((3,)), dma((3,)), dma((8,)), dma((8,)),
+            v(M, F), v(M, F), v(G, F), v(2, 2, 4, 4, 2, 64, 128), v(2, 2 * F, F, dtype=F32),
+            dma((3,)), dma((3,)), dma((2,)), dma((4,)),
         ],
         compiler_params=pltpu.CompilerParams(vmem_limit_bytes=58 * 2**20),
         name="results",

time: 96.1 us -> 86.6 us (0.901); the launches traced: 94.6 us -> 86.5 us
  Pallas kernels: 94 us -> 85.7 us
    pallas_call x1, Pallas kernels: 89.3 us -> 81.4 us  [shards(): pl.pallas_call(body, out_shape=(jax.ShapeDtypeStruct((M, F), BF), jax.Sha...]
where the time goes in v5:
time: 86.6 us; the launch traced here: 86.5 us
  Pallas kernels  85.7 us (99%)
    pallas_call x1, Pallas kernels, shards(): pl.pallas_call(body, out_shape=(jax.ShapeDtypeStruct((M, F), BF), jax.Sha...  81.4 us
    pallas_call x1, Pallas kernels, shards(): pl.pallas_call(write_results, out_shape=(jax.ShapeDtypeStruct((M, F), BF)...  4.29 us

profile of v5, /device:TPU:1, one launch (start us, length us, event | category | flops | bytes accessed | tf_op | source)
XLA Modules:
  0.0 86.5 jit_solution(14649113849319078516)
XLA Ops:
  0.6 81.4 %encoder.1 = (bf16[128,512]{1,0:T(8,128)(2,1)}, bf16[128,512]{1,0:T(8,128)(2,1)}, bf16[2048,512]{1,0:T(8,128)(2,1)}, bf16[2,2,4,4,2,64,128]{6,5,4,3,2,1,0:T(8,128)(2,1)}) custom-call(bf16[2048,512]{1,0:T(8,128)(2,1)} %grid_in.1, bf16[128,512]{1,0:T(8,128)(2,1)} %mesh_in.1, s32[16,128]{1,0:T(8,128)} %bitcast.2, s32[1,128]{1,0:T(1,128)} %bitcast.3, s32[16]{0:T(128)} %off.1, ...), custom_call_target="tpu_custom_call" | custom-call | tf_op jit(solution)/shard_map/encoder/pallas_call | solution.py:628
  82.0 4.3 %results.1 = (bf16[128,512]{1,0:T(8,128)(2,1)}, bf16[128,512]{1,0:T(8,128)(2,1)}, bf16[2048,512]{1,0:T(8,128)(2,1)}, f32[2,1024,512]{2,1,0:T(8,128)}) custom-call(bf16[128,512]{1,0:T(8,128)(2,1)} %get-tuple-element.8.enc, bf16[128,512]{1,0:T(8,128)(2,1)} %get-tuple-element.9.mesh_o, bf16[2048,512]{1,0:T(8,128)(2,1)} %get-tuple-element.10.gg, ...), custom_call_target="tpu_custom_call" | custom-call | tf_op jit(solution)/shard_map/results/pallas_call | solution.py:648

commit v6 on v5

--- a/solution.py
+++ b/solution.py
@@ -28,9 +28,9 @@
 
 (
     E1M, E1C, HUP, HDOWN, E2, E3A, E3B, E4, E5, E6, KUP, KDOWN, E8, GUP, GDOWN,
-    RS3, RS3P, AG1, WY, WR, WF, PRE, RS1, RS2, AG2, AG3, AGF,
-) = list(range(19)) + [20, 26, 34, 36, 42, 48, 54, 60]
-N_REMOTE = 68
+    RS3, RS3P, E2D, WY, WR, WF, PRE, RS1, RS2, AG2, AG3, AGF,
+) = list(range(19)) + [20, 26, 34, 42, 48, 54, 68, 74]
+N_REMOTE = 82
 
 
 def dot(a, b):
@@ -109,7 +109,7 @@
         c.start()
 
     first = [partner, (across, o), (across, g), (sib, g), (far, g)]
-    first += [(along(axis, d), g) for axis in range(2) for d in (1, 2, 3)]
+    first += [(along(axis, d) + y * (across - s), g) for axis in range(2) for d in (1, 2, 3) for y in range(2)]
     barrier = pltpu.get_barrier_semaphore()
     for dev in first:
         pl.semaphore_signal(barrier, inc=1, device_id=dev, device_id_type=MESH)
@@ -183,27 +183,27 @@
         xs[pl.ds(pl.multiple_of(t * 512, 512), 512), :] = dot(hot, wide[...]).astype(BF)
         return carry
 
-    lax.fori_loop(0, 3, gather, 0)
+    lax.fori_loop(0, 2, gather, 0)
 
     for n in (0, 1, 2, 3):
         loads[n].wait()
-    qa = dot(mf[0], wq[0])
-    da = dot_t(cf[0], wo[0])
     loads[4].wait()
     loads[5].wait()
+    qa = dot(mf[0], wq[0])
     e1m.wait_recv()
+    qd[0, 0] = (qa + dot(mf[1], wq[1])).astype(BF)
+    e2 = remote(qd.at[0, 0], qd.at[1, 0], E2, partner)
+    e2.start()
+    da = dot_t(cf[0], wo[0])
     e1c.wait_recv()
-    qa = qa + dot(mf[1], wq[1])
-    da = da + dot_t(cf[1], wo[1])
-    qd[0, 0] = qa.astype(BF)
-    qd[0, 1] = da.astype(BF)
-    e2 = remote(qd.at[0], qd.at[1], E2, partner)
-    e2.start()
+    qd[0, 1] = (da + dot_t(cf[1], wo[1])).astype(BF)
+    e2d = remote(qd.at[0, 1], qd.at[1, 1], E2D, partner)
+    e2d.start()
     for n, (_, c) in enumerate(wring):
         c.wait_recv()
         wfwd[n + 1 + n // 3].start()
 
-    lax.fori_loop(3, 4, gather, 0)
+    lax.fori_loop(2, 4, gather, 0)
 
     def turn(side):
         for k in range(2):
@@ -247,6 +247,7 @@
     scores(0)
     e3a.start()
     e2.wait_recv()
+    e2d.wait_recv()
     turn(1)
     for c in wback:
         c.wait_recv()
@@ -311,13 +312,25 @@
                     gb[k, 1, x, 2 * f + y] = out[64:, f * 128 : (f + 1) * 128]
         return carry
 
+    line = (at_z, at_x)
+    axis_of = (1, 0)
+
+    def ring(h, stage, d):
+        return (along(axis_of[h] if stage == 1 else 1 - axis_of[h], d), g)
+
+    def ahead(n, d):
+        return (n + d) % 4
+
     weight_terms(0, 0)
     presum = [
-        remote(gb.at[1 - core, n], pre.at[n], PRE + n, (sib, g))
-        for n in range(2)
+        remote(gb.at[1 - core, h, ahead(line[h], d)], pre.at[h, ahead(line[h], d)], PRE + 4 * h + d, (sib, g))
+        for h in range(2)
+        for d in range(4)
     ]
-    for c in presum:
-        c.start()
+    order = [0, 1, 2, 4, 5, 6, 3, 7]
+    order = [(n // 4, (n % 4 + 1) % 4) for n in order]
+    for h, d in order:
+        presum[4 * h + d].start()
     for a in range(2):
         z4 = zy[1, HL + a * 4 : HL + a * 4 + 4].reshape(4 * M, F)
         att_send[:, a * 256 : (a + 1) * 256] = diagonal(
@@ -333,26 +346,17 @@
         )
 
 
-    line = (at_z, at_x)
-    axis_of = (1, 0)
-
-    def ring(h, stage, d):
-        return (along(axis_of[h] if stage == 1 else 1 - axis_of[h], d), g)
-
-    def ahead(n, d):
-        return (n + d) % 4
-
     stage1 = [
         remote(gb.at[core, h, ahead(line[h], d)], rs1.at[h, d - 1], RS1 + 3 * h + d - 1, ring(h, 1, d))
         for h in range(2)
         for d in (1, 2, 3)
     ]
-    for h in range(2):
-        presum[h].wait_recv()
-        for n in range(4):
-            gb[core, h, n] = (gb[core, h, n].astype(F32) + pre[h, n].astype(F32)).astype(BF)
-        for c in stage1[3 * h : 3 * h + 3]:
-            c.start()
+    for h, d in order:
+        presum[4 * h + d].wait_recv()
+        n = ahead(line[h], d)
+        gb[core, h, n] = (gb[core, h, n].astype(F32) + pre[h, n].astype(F32)).astype(BF)
+        if d:
+            stage1[3 * h + d - 1].start()
 
     e4.wait_recv()
     att = (att_own[...] + att_recv[...].astype(F32)).astype(BF)
@@ -372,6 +376,19 @@
 
     lax.fori_loop(0, 8, edge_grads, 0, unroll=2)
 
+    def rows_of(first, count):
+        hot = jnp.where(
+            (iota((count, G), 0) + first).astype(F32) == srow[0:1, :], 1.0, 0.0
+        ).astype(BF)
+        return dot(hot, gedge[...])
+
+    halo_send[0] = rows_of(0, RIM).astype(BF)
+    halo_send[1] = rows_of(RIM + G, RIM).astype(BF)
+    gdown = remote(halo_send.at[0], halo_recv.at[1], GDOWN, (down, g))
+    gup = remote(halo_send.at[1], halo_recv.at[0], GUP, (up, g))
+    gdown.start()
+    gup.start()
+
     e5.wait_recv()
     enc = (mf[0].astype(F32) + enc_own[...] + enc_recv[...].astype(F32)).astype(BF)
     ef[0] = enc
@@ -379,19 +396,6 @@
     e6.start()
     enc_copy = pltpu.make_async_copy(ef.at[0], enc_out, osem.at[0])
     enc_copy.start()
-
-    def rows_of(first, count):
-        hot = jnp.where(
-            (iota((count, G), 0) + first).astype(F32) == srow[0:1, :], 1.0, 0.0
-        ).astype(BF)
-        return dot(hot, gedge[...])
-
-    halo_send[0] = rows_of(0, RIM).astype(BF)
-    halo_send[1] = rows_of(RIM + G, RIM).astype(BF)
-    gdown = remote(halo_send.at[0], halo_recv.at[1], GDOWN, (down, g))
-    gup = remote(halo_send.at[1], halo_recv.at[0], GUP, (up, g))
-    gdown.start()
-    gup.start()
 
     stage2 = [
         remote(
@@ -457,26 +461,27 @@
 
     block = (tp[...].astype(F32) + rec[...].astype(F32)).reshape(128, 128).T.astype(BF)
 
-    bq[0, ylo] = block[:64]
-    bq[1, ylo] = block[64:]
-    back1 = remote(bq.at[:, ylo], bq.at[:, ylo], AG1, (across, g))
-    back1.start()
-    lax.fori_loop(2, 3, interior, 0)
-    remote(bq.at[:, 1 - ylo], bq.at[:, 1 - ylo], AG1, (across, g)).wait_recv()
-
+    bq[0] = block[:64]
+    bq[1] = block[64:]
     back2, back2_in, back3, back3_in = [], [], [], []
     for h in range(2):
+        for d in range(4):
+            to, of = ring(h, 2, d)[0], ahead(line[1 - h], 4 - d)
+            for y in range(2):
+                if d or y:
+                    n = AG2 + 7 * h + 2 * d + y - 1
+                    back2.append(remote(bq.at[h], bp.at[h, line[1 - h], ylo], n, (to + y * (across - s), g)))
+                    came = bp.at[h, of, ylo + y * (1 - 2 * ylo)]
+                    back2_in.append(remote(bq.at[h], came, n, partner))
         for d in (1, 2, 3):
-            n = 3 * h + d - 1
-            from2, from3 = ahead(line[1 - h], 4 - d), ahead(line[h], 4 - d)
-            back2.append(remote(bq.at[h], bp.at[h, line[1 - h]], AG2 + n, ring(h, 2, d)))
-            back2_in.append(remote(bq.at[h], bp.at[h, from2], AG2 + n, partner))
-            back3.append(remote(bp.at[h], blocks.at[core, h, line[h]], AG3 + n, ring(h, 1, d)))
-            back3_in.append(remote(bp.at[h], blocks.at[core, h, from3], AG3 + n, partner))
+            n = AG3 + 3 * h + d - 1
+            back3.append(remote(bp.at[h], blocks.at[core, h, line[h]], n, ring(h, 1, d)))
+            back3_in.append(remote(bp.at[h], blocks.at[core, h, ahead(line[h], 4 - d)], n, partner))
     for c in back2:
         c.start()
     for h in range(2):
-        bp[h, line[1 - h]] = bq[h]
+        bp[h, line[1 - h], ylo] = bq[h]
+    lax.fori_loop(2, 3, interior, 0)
 
     where_n = iota((M, 256), 1) - R
     delta = where_n - iota((M, 256), 0)
@@ -508,7 +513,7 @@
     mo_own[...] = dot(matt, wmo[0])
 
     for h in range(2):
-        for c in back2_in[3 * h : 3 * h + 3]:
+        for c in back2_in[7 * h : 7 * h + 7]:
             c.wait_recv()
         for c in back3[3 * h : 3 * h + 3]:
             c.start()
@@ -538,7 +543,7 @@
     gg_copy = pltpu.make_async_copy(ggs, gg_out, osem.at[2])
     gg_copy.start()
 
-    singles = [e1m, e1c, hup, hdown, e2, e3a, e3b, e4, e5, e6, kup, kdown, gdown, gup, stage3, back1]
+    singles = [e1m, e1c, hup, hdown, e2, e2d, e3a, e3b, e4, e5, e6, kup, kdown, gdown, gup, stage3]
     for c in singles + wy + [c for c, _ in wring] + wfwd + presum + stage1 + stage2 + back2:
         c.wait_send()
     e8.wait()
@@ -621,7 +626,7 @@
         gedge=v(G, F), halo_send=v(2, RIM, F), halo_recv=v(2, RIM, F), ggs=v(G, F),
         gb=v(2, 2, 4, 8, 64, 128), pre=v(2, 4, 8, 64, 128), rs1=v(2, 3, 8, 64, 128), rsum=v(2, 8, 64, 128),
         rs2=v(2, 3, 2, 64, 128), tt=v(2, 2, 64, 128), tp=v(2, 64, 128), rec=v(2, 64, 128),
-        bq=v(2, 2, 64, 128), bp=v(2, 4, 2, 64, 128), blocks=v(2, 2, 4, 4, 2, 64, 128),
+        bq=v(2, 64, 128), bp=v(2, 4, 2, 64, 128), blocks=v(2, 2, 4, 4, 2, 64, 128),
         lsem=dma((12,)), osem=dma((4,)), ssem=dma((N_REMOTE,)), rsem=dma((N_REMOTE,)),
         out_s=dma((2, 8)),
     )

time: 86.6 us -> 82.9 us (0.957)
  Pallas kernels: 85.7 us -> 81.9 us
    pallas_call x1, Pallas kernels: 81.4 us -> 77.6 us  [shards(): pl.pallas_call(body, out_shape=(jax.ShapeDtypeStruct((M, F), BF), jax.Sha...]
where the time goes in v6:
time: 82.9 us; the launch traced here: 82.7 us
  Pallas kernels  81.9 us (99%)
    pallas_call x1, Pallas kernels, shards(): pl.pallas_call(body, out_shape=(jax.ShapeDtypeStruct((M, F), BF), jax.Sha...  77.6 us
    pallas_call x1, Pallas kernels, shards(): pl.pallas_call(write_results, out_shape=(jax.ShapeDtypeStruct((M, F), BF)...  4.29 us

profile of v6, /device:TPU:1, one launch (start us, length us, event | category | flops | bytes accessed | tf_op | source)
XLA Modules:
  0.0 82.7 jit_solution(7049382292185968328)
XLA Ops:
  0.6 77.6 %encoder.1 = (bf16[128,512]{1,0:T(8,128)(2,1)}, bf16[128,512]{1,0:T(8,128)(2,1)}, bf16[2048,512]{1,0:T(8,128)(2,1)}, bf16[2,2,4,4,2,64,128]{6,5,4,3,2,1,0:T(8,128)(2,1)}) custom-call(bf16[2048,512]{1,0:T(8,128)(2,1)} %grid_in.1, bf16[128,512]{1,0:T(8,128)(2,1)} %mesh_in.1, s32[16,128]{1,0:T(8,128)} %bitcast.2, s32[1,128]{1,0:T(1,128)} %bitcast.3, s32[16]{0:T(128)} %off.1, ...), custom_call_target="tpu_custom_call" | custom-call | tf_op jit(solution)/shard_map/encoder/pallas_call | solution.py:633
  78.3 4.3 %results.1 = (bf16[128,512]{1,0:T(8,128)(2,1)}, bf16[128,512]{1,0:T(8,128)(2,1)}, bf16[2048,512]{1,0:T(8,128)(2,1)}, f32[2,1024,512]{2,1,0:T(8,128)}) custom-call(bf16[128,512]{1,0:T(8,128)(2,1)} %get-tuple-element.8.enc, bf16[128,512]{1,0:T(8,128)(2,1)} %get-tuple-element.9.mesh_o, bf16[2048,512]{1,0:T(8,128)(2,1)} %get-tuple-element.10.gg, ...), custom_call_target="tpu_custom_call" | custom-call | tf_op jit(solution)/shard_map/results/pallas_call | solution.py:653

commit v7 on v6

--- a/solution.py
+++ b/solution.py
@@ -240,7 +240,7 @@
             sd_send[side, t] = total.astype(BF)
             return carry
 
-        lax.fori_loop(0, 8, step, 0, unroll=2)
+        lax.fori_loop(0, 8, step, 0, unroll=4)
 
     e3a = remote(sd_send.at[0], sd_recv.at[1], E3A, partner)
     e3b = remote(sd_send.at[1], sd_recv.at[0], E3B, partner)
@@ -284,7 +284,7 @@
         zy[:, :, pl.ds(pl.multiple_of(t * 16, 16), 16), :] = out.reshape(2, 16, 16, F)
         return carry
 
-    lax.fori_loop(0, 8, sums, 0, unroll=2)
+    lax.fori_loop(0, 8, sums, 0, unroll=4)
 
     def diagonal(x):
         x = x.reshape(4, M, 256)
@@ -481,7 +481,30 @@
         c.start()
     for h in range(2):
         bp[h, line[1 - h], ylo] = bq[h]
-    lax.fori_loop(2, 3, interior, 0)
+    lax.fori_loop(2, 4, interior, 0)
+
+    for h in range(2):
+        for c in back2_in[7 * h : 7 * h + 7]:
+            c.wait_recv()
+        for c in back3[3 * h : 3 * h + 3]:
+            c.start()
+        blocks[core, h, line[h]] = bp[h]
+
+    def pass_copy(k, h, d):
+        part = blocks.at[k, h, ahead(line[h], 4 - d)]
+        return remote(part, part, AGF + 4 * h + d, (sib, g))
+
+    def result_copy(k, h, d):
+        n = ahead(line[h], 4 - d)
+        return pltpu.make_async_copy(blocks.at[k, h, n], gkv_out.at[k, h, n], out_s.at[k, 4 * h + d])
+
+    passed = [pass_copy(core, h, d) for h in range(2) for d in range(4)]
+    handed = [pass_copy(1 - core, h, d) for h in range(2) for d in range(4)]
+    mine_out = [result_copy(core, h, d) for h in range(2) for d in range(4)]
+    other_out = [result_copy(1 - core, h, d) for h in range(2) for d in range(4)]
+    for n in (0, 4):
+        passed[n].start()
+        mine_out[n].start()
 
     where_n = iota((M, 256), 1) - R
     delta = where_n - iota((M, 256), 0)
@@ -512,30 +535,6 @@
     e8.start()
     mo_own[...] = dot(matt, wmo[0])
 
-    for h in range(2):
-        for c in back2_in[7 * h : 7 * h + 7]:
-            c.wait_recv()
-        for c in back3[3 * h : 3 * h + 3]:
-            c.start()
-        blocks[core, h, line[h]] = bp[h]
-
-    def pass_copy(k, h, d):
-        part = blocks.at[k, h, ahead(line[h], 4 - d)]
-        return remote(part, part, AGF + 4 * h + d, (sib, g))
-
-    def result_copy(k, h, d):
-        n = ahead(line[h], 4 - d)
-        return pltpu.make_async_copy(blocks.at[k, h, n], gkv_out.at[k, h, n], out_s.at[k, 4 * h + d])
-
-    passed = [pass_copy(core, h, d) for h in range(2) for d in range(4)]
-    handed = [pass_copy(1 - core, h, d) for h in range(2) for d in range(4)]
-    mine_out = [result_copy(core, h, d) for h in range(2) for d in range(4)]
-    other_out = [result_copy(1 - core, h, d) for h in range(2) for d in range(4)]
-    for n in (0, 4):
-        passed[n].start()
-        mine_out[n].start()
-
-    lax.fori_loop(3, 4, interior, 0)
     gdown.wait_recv()
     gup.wait_recv()
     ggs[0:RIM, :] = (ggs[0:RIM, :].astype(F32) + halo_recv[0].astype(F32)).astype(BF)
@@ -546,16 +545,16 @@
     singles = [e1m, e1c, hup, hdown, e2, e2d, e3a, e3b, e4, e5, e6, kup, kdown, gdown, gup, stage3]
     for c in singles + wy + [c for c, _ in wring] + wfwd + presum + stage1 + stage2 + back2:
         c.wait_send()
-    e8.wait()
-    mo_val[...] = (ef[0].astype(F32) + mo_own[...] + mo_recv[...].astype(F32)).astype(BF)
-    mo_copy = pltpu.make_async_copy(mo_val, mesh_out, osem.at[3])
-    mo_copy.start()
-
     for d in (1, 2, 3):
         for h in range(2):
             back3_in[3 * h + d - 1].wait_recv()
             passed[4 * h + d].start()
             mine_out[4 * h + d].start()
+    e8.wait()
+    mo_val[...] = (ef[0].astype(F32) + mo_own[...] + mo_recv[...].astype(F32)).astype(BF)
+    mo_copy = pltpu.make_async_copy(mo_val, mesh_out, osem.at[3])
+    mo_copy.start()
+
     for c in back3:
         c.wait_send()
     for d in range(4):
@@ -576,11 +575,14 @@
     g = lax.axis_index("head")
     loads = [pltpu.make_async_copy(gkv.at[k], low.at[k], k_in.at[k]) for k in range(2)]
     others = [pltpu.make_async_copy(a, b, s_in.at[n]) for n, (a, b, _) in enumerate(plain)]
-    for c in loads + others:
+    for c in loads:
         c.start()
     stores = []
     for k in range(2):
         loads[k].wait()
+        if k == 0:
+            for c in others[::-1]:
+                c.start()
         for n in range(2):
             half = g if n == 0 else 1 - g
             for x in (2 * n, 2 * n + 1):

time: 82.9 us -> 84.1 us (1.014)
  Pallas kernels: 81.9 us -> 83.1 us
    pallas_call x1, Pallas kernels: 4.29 us -> 5.88 us  [shards(): pl.pallas_call(write_results, out_shape=(jax.ShapeDtypeStruct((M, F), BF)...]
where the time goes in v7:
time: 84.1 us; the launch traced here: 83.9 us
  Pallas kernels  83.1 us (99%)
    pallas_call x1, Pallas kernels, shards(): pl.pallas_call(body, out_shape=(jax.ShapeDtypeStruct((M, F), BF), jax.Sha...  77.2 us
    pallas_call x1, Pallas kernels, shards(): pl.pallas_call(write_results, out_shape=(jax.ShapeDtypeStruct((M, F), BF)...  5.88 us

profile of v7, /device:TPU:1, one launch (start us, length us, event | category | flops | bytes accessed | tf_op | source)
XLA Modules:
  0.0 83.9 jit_solution(11200602901236399782)
XLA Ops:
  0.6 77.2 %encoder.1 = (bf16[128,512]{1,0:T(8,128)(2,1)}, bf16[128,512]{1,0:T(8,128)(2,1)}, bf16[2048,512]{1,0:T(8,128)(2,1)}, bf16[2,2,4,4,2,64,128]{6,5,4,3,2,1,0:T(8,128)(2,1)}) custom-call(bf16[2048,512]{1,0:T(8,128)(2,1)} %grid_in.1, bf16[128,512]{1,0:T(8,128)(2,1)} %mesh_in.1, s32[16,128]{1,0:T(8,128)} %bitcast.2, s32[1,128]{1,0:T(1,128)} %bitcast.3, s32[16]{0:T(128)} %off.1, ...), custom_call_target="tpu_custom_call" | custom-call | tf_op jit(solution)/shard_map/encoder/pallas_call | solution.py:635
  77.8 5.9 %results.1 = (bf16[128,512]{1,0:T(8,128)(2,1)}, bf16[128,512]{1,0:T(8,128)(2,1)}, bf16[2048,512]{1,0:T(8,128)(2,1)}, f32[2,1024,512]{2,1,0:T(8,128)}) custom-call(bf16[128,512]{1,0:T(8,128)(2,1)} %get-tuple-element.8.enc, bf16[128,512]{1,0:T(8,128)(2,1)} %get-tuple-element.9.mesh_o, bf16[2048,512]{1,0:T(8,128)(2,1)} %get-tuple-element.10.gg, ...), custom_call_target="tpu_custom_call" | custom-call | tf_op jit(solution)/shard_map/results/pallas_call | solution.py:655

commit v8 on v7

--- a/solution.py
+++ b/solution.py
@@ -438,17 +438,7 @@
     def _():
         stage3p.start()
 
-    loads[8].wait()
-    loads[9].wait()
-    e6.wait_recv()
-    for k in range(2):
-        mkv[k, R : R + M, :] = (dot(ef[0], wm[0, 1 + k]) + dot(ef[1], wm[1, 1 + k])).astype(BF)
-    kup = remote(mkv.at[:, pl.ds(M, R), :], mkv.at[:, pl.ds(0, R), :], KUP, (up, g))
-    kdown = remote(mkv.at[:, pl.ds(R, R), :], mkv.at[:, pl.ds(R + M, R), :], KDOWN, (down, g))
-    kup.start()
-    kdown.start()
-    mq[...] = (dot(ef[0], wm[0, 0]) + dot(ef[1], wm[1, 0])).astype(BF)
-
+    lax.fori_loop(2, 3, interior, 0)
     stage3.wait_recv()
 
     @pl.when(late == 0)
@@ -481,7 +471,18 @@
         c.start()
     for h in range(2):
         bp[h, line[1 - h], ylo] = bq[h]
-    lax.fori_loop(2, 4, interior, 0)
+    loads[8].wait()
+    loads[9].wait()
+    e6.wait_recv()
+    for k in range(2):
+        mkv[k, R : R + M, :] = (dot(ef[0], wm[0, 1 + k]) + dot(ef[1], wm[1, 1 + k])).astype(BF)
+    kup = remote(mkv.at[:, pl.ds(M, R), :], mkv.at[:, pl.ds(0, R), :], KUP, (up, g))
+    kdown = remote(mkv.at[:, pl.ds(R, R), :], mkv.at[:, pl.ds(R + M, R), :], KDOWN, (down, g))
+    kup.start()
+    kdown.start()
+    mq[...] = (dot(ef[0], wm[0, 0]) + dot(ef[1], wm[1, 0])).astype(BF)
+
+    lax.fori_loop(3, 4, interior, 0)
 
     for h in range(2):
         for c in back2_in[7 * h : 7 * h + 7]:
@@ -575,14 +576,11 @@
     g = lax.axis_index("head")
     loads = [pltpu.make_async_copy(gkv.at[k], low.at[k], k_in.at[k]) for k in range(2)]
     others = [pltpu.make_async_copy(a, b, s_in.at[n]) for n, (a, b, _) in enumerate(plain)]
-    for c in loads:
+    for c in loads + others:
         c.start()
     stores = []
     for k in range(2):
         loads[k].wait()
-        if k == 0:
-            for c in others[::-1]:
-                c.start()
         for n in range(2):
             half = g if n == 0 else 1 - g
             for x in (2 * n, 2 * n + 1):

time: 84.1 us -> 82.1 us (0.976)
  Pallas kernels: 83.1 us -> 81.1 us
    pallas_call x1, Pallas kernels: 5.88 us -> 4.29 us  [shards(): pl.pallas_call(write_results, out_shape=(jax.ShapeDtypeStruct((M, F), BF)...]
where the time goes in v8:
time: 82.1 us; the launch traced here: 81.9 us
  Pallas kernels  81.1 us (99%)
    pallas_call x1, Pallas kernels, shards(): pl.pallas_call(body, out_shape=(jax.ShapeDtypeStruct((M, F), BF), jax.Sha...  76.8 us
    pallas_call x1, Pallas kernels, shards(): pl.pallas_call(write_results, out_shape=(jax.ShapeDtypeStruct((M, F), BF)...  4.29 us

profile of v8, /device:TPU:1, one launch (start us, length us, event | category | flops | bytes accessed | tf_op | source)
XLA Modules:
  0.0 81.9 jit_solution(14911168344805673434)
XLA Ops:
  0.6 76.8 %encoder.1 = (bf16[128,512]{1,0:T(8,128)(2,1)}, bf16[128,512]{1,0:T(8,128)(2,1)}, bf16[2048,512]{1,0:T(8,128)(2,1)}, bf16[2,2,4,4,2,64,128]{6,5,4,3,2,1,0:T(8,128)(2,1)}) custom-call(bf16[2048,512]{1,0:T(8,128)(2,1)} %grid_in.1, bf16[128,512]{1,0:T(8,128)(2,1)} %mesh_in.1, s32[16,128]{1,0:T(8,128)} %bitcast.2, s32[1,128]{1,0:T(1,128)} %bitcast.3, s32[16]{0:T(128)} %off.1, ...), custom_call_target="tpu_custom_call" | custom-call | tf_op jit(solution)/shard_map/encoder/pallas_call | solution.py:633
  77.5 4.3 %results.1 = (bf16[128,512]{1,0:T(8,128)(2,1)}, bf16[128,512]{1,0:T(8,128)(2,1)}, bf16[2048,512]{1,0:T(8,128)(2,1)}, f32[2,1024,512]{2,1,0:T(8,128)}) custom-call(bf16[128,512]{1,0:T(8,128)(2,1)} %get-tuple-element.8.enc, bf16[128,512]{1,0:T(8,128)(2,1)} %get-tuple-element.9.mesh_o, bf16[2048,512]{1,0:T(8,128)(2,1)} %get-tuple-element.10.gg, ...), custom_call_target="tpu_custom_call" | custom-call | tf_op jit(solution)/shard_map/results/pallas_call | solution.py:653

commit v9 on v8

--- a/solution.py
+++ b/solution.py
@@ -262,7 +262,7 @@
     dlane = dot(dg, tile)
     live = iota((8, K, 128), 1).astype(F32) < dlane[:, None, :]
 
-    for side in (1, 0):
+    def softmax(side):
         (e3a if side else e3b).wait_recv()
         raw = (sd[side, :, :, :128] + sd_recv[side, :, :, :128].astype(F32)) * SCALE
         dp = sd[side, :, :, 128:] + sd_recv[side, :, :, 128:].astype(F32)
@@ -275,16 +275,19 @@
         pb[:, :, a : a + 128] = dr.astype(BF)
         pb[:, :, 256 + a : 256 + a + 128] = prob.astype(BF)
 
-    def sums(t, carry):
-        xg = xs[pl.ds(pl.multiple_of(t * 256, 256), 256), :]
-        same = (iota((512, 256), 0) & 15) == iota((512, 256), 1) // 16
-        sel = jnp.where(iota((K, 256), 0) == (iota((K, 256), 1) & 15), 1.0, 0.0).astype(BF)
-        pt = jnp.where(same, dot_first(pb[t], sel), 0.0).astype(BF)
-        out = dot(pt, xg).astype(BF)
-        zy[:, :, pl.ds(pl.multiple_of(t * 16, 16), 16), :] = out.reshape(2, 16, 16, F)
-        return carry
-
-    lax.fori_loop(0, 8, sums, 0, unroll=4)
+    def sums(side):
+        def step(t, carry):
+            xg = xs[pl.ds(pl.multiple_of(t * 256, 256), 256), :]
+            same = (iota((256, 256), 0) & 15) == iota((256, 256), 1) // 16
+            sel = jnp.where(iota((K, 256), 0) == (iota((K, 256), 1) & 15), 1.0, 0.0).astype(BF)
+            a = side * 128
+            both = jnp.concatenate([pb[t, :, a : a + 128], pb[t, :, 256 + a : 256 + a + 128]], axis=1)
+            pt = jnp.where(same, dot_first(both, sel), 0.0).astype(BF)
+            out = dot(pt, xg).astype(BF).reshape(2, HL, 16, F)
+            zy[:, side * HL : side * HL + HL, pl.ds(pl.multiple_of(t * 16, 16), 16), :] = out
+            return carry
+
+        lax.fori_loop(0, 8, step, 0, unroll=4)
 
     def diagonal(x):
         x = x.reshape(4, M, 256)
@@ -294,23 +297,21 @@
             out = out + jnp.where(head == i, x[i], 0.0)
         return out
 
-    def weight_terms(n, carry):
+    def weight_terms(n, side):
         k = (1 - core) + n * (2 * core - 1)
-        for side in range(2):
-            for p in range(4):
-                xt = qdt[side, k, p * 128 : (p + 1) * 128, :].astype(F32)
-                first = iota((128, M), 0) < 64
-                lhs = jnp.concatenate(
-                    [jnp.where(first, xt, 0.0).astype(BF), jnp.where(first, 0.0, xt).astype(BF)], axis=1
-                )
-                h = side * HL + 2 * p
-                rhs = zy[k, h : h + 2].reshape(2 * M, F)
-                out = dot(lhs, rhs).astype(BF)
-                for f in range(4):
-                    x, y = 2 * side + p // 2, p % 2
-                    gb[k, 0, f, 2 * x + y] = out[:64, f * 128 : (f + 1) * 128]
-                    gb[k, 1, x, 2 * f + y] = out[64:, f * 128 : (f + 1) * 128]
-        return carry
+        for p in range(4):
+            xt = qdt[side, k, p * 128 : (p + 1) * 128, :].astype(F32)
+            first = iota((128, M), 0) < 64
+            lhs = jnp.concatenate(
+                [jnp.where(first, xt, 0.0).astype(BF), jnp.where(first, 0.0, xt).astype(BF)], axis=1
+            )
+            h = side * HL + 2 * p
+            rhs = zy[k, h : h + 2].reshape(2 * M, F)
+            out = dot(lhs, rhs).astype(BF)
+            for f in range(4):
+                x, y = 2 * side + p // 2, p % 2
+                gb[k, 0, f, 2 * x + y] = out[:64, f * 128 : (f + 1) * 128]
+                gb[k, 1, x, 2 * f + y] = out[64:, f * 128 : (f + 1) * 128]
 
     line = (at_z, at_x)
     axis_of = (1, 0)
@@ -321,6 +322,19 @@
     def ahead(n, d):
         return (n + d) % 4
 
+    softmax(1)
+    sums(1)
+    for a in range(2):
+        z4 = zy[1, HL + a * 4 : HL + a * 4 + 4].reshape(4 * M, F)
+        att_send[:, a * 256 : (a + 1) * 256] = diagonal(
+            dot(z4, wkv_oth[1, :, a * 256 : (a + 1) * 256])
+        ).astype(BF)
+    e4 = remote(att_send, att_recv, E4, partner)
+    e4.start()
+    weight_terms(0, 1)
+    weight_terms(1, 1)
+    softmax(0)
+    sums(0)
     weight_terms(0, 0)
     presum = [
         remote(gb.at[1 - core, h, ahead(line[h], d)], pre.at[h, ahead(line[h], d)], PRE + 4 * h + d, (sib, g))
@@ -331,13 +345,6 @@
     order = [(n // 4, (n % 4 + 1) % 4) for n in order]
     for h, d in order:
         presum[4 * h + d].start()
-    for a in range(2):
-        z4 = zy[1, HL + a * 4 : HL + a * 4 + 4].reshape(4 * M, F)
-        att_send[:, a * 256 : (a + 1) * 256] = diagonal(
-            dot(z4, wkv_oth[1, :, a * 256 : (a + 1) * 256])
-        ).astype(BF)
-    e4 = remote(att_send, att_recv, E4, partner)
-    e4.start()
     weight_terms(1, 0)
     for a in range(2):
         z4 = zy[1, a * 4 : a * 4 + 4].reshape(4 * M, F)

time: 82.1 us -> 78.9 us (0.961)
  Pallas kernels: 81.1 us -> 78 us
    pallas_call x1, Pallas kernels: 76.8 us -> 73.7 us  [shards(): pl.pallas_call(body, out_shape=(jax.ShapeDtypeStruct((M, F), BF), jax.Sha...]
where the time goes in v9:
time: 78.9 us; the launch traced here: 78.8 us
  Pallas kernels  78 us (99%)
  between operations  0.8 us (1%)
    pallas_call x1, Pallas kernels, shards(): pl.pallas_call(body, out_shape=(jax.ShapeDtypeStruct((M, F), BF), jax.Sha...  73.7 us
    pallas_call x1, Pallas kernels, shards(): pl.pallas_call(write_results, out_shape=(jax.ShapeDtypeStruct((M, F), BF)...  4.29 us

profile of v9, /device:TPU:1, one launch (start us, length us, event | category | flops | bytes accessed | tf_op | source)
XLA Modules:
  0.0 78.8 jit_solution(9218837842869188351)
XLA Ops:
  0.6 73.7 %encoder.1 = (bf16[128,512]{1,0:T(8,128)(2,1)}, bf16[128,512]{1,0:T(8,128)(2,1)}, bf16[2048,512]{1,0:T(8,128)(2,1)}, bf16[2,2,4,4,2,64,128]{6,5,4,3,2,1,0:T(8,128)(2,1)}) custom-call(bf16[2048,512]{1,0:T(8,128)(2,1)} %grid_in.1, bf16[128,512]{1,0:T(8,128)(2,1)} %mesh_in.1, s32[16,128]{1,0:T(8,128)} %bitcast.2, s32[1,128]{1,0:T(1,128)} %bitcast.3, s32[16]{0:T(128)} %off.1, ...), custom_call_target="tpu_custom_call" | custom-call | tf_op jit(solution)/shard_map/encoder/pallas_call | solution.py:640
  74.3 4.3 %results.1 = (bf16[128,512]{1,0:T(8,128)(2,1)}, bf16[128,512]{1,0:T(8,128)(2,1)}, bf16[2048,512]{1,0:T(8,128)(2,1)}, f32[2,1024,512]{2,1,0:T(8,128)}) custom-call(bf16[128,512]{1,0:T(8,128)(2,1)} %get-tuple-element.8.enc, bf16[128,512]{1,0:T(8,128)(2,1)} %get-tuple-element.9.mesh_o, bf16[2048,512]{1,0:T(8,128)(2,1)} %get-tuple-element.10.gg, ...), custom_call_target="tpu_custom_call" | custom-call | tf_op jit(solution)/shard_map/results/pallas_call | solution.py:660
